TPU v7x, 256 devices: a whole 4x4x8 slice. The times are simulated.
256 devices in a mesh: rep: 4 (over x_hi, core), cplx: 4 (over y), row: 16 (over x_lo, z).
Axes of the slice: x: 4 (x_hi: 2, x_lo: 2; x = x_hi * 2 + x_lo), y: 4, z: 8, core: 2. Of those that a mesh axis runs over, the one named last changes fastest.
Arguments:
- pair_map: bfloat16 [16, 128, 128, 128], P(('rep', 'cplx'), 'row'), may hold values from -6 to 6
- cotangent: bfloat16 [16, 128, 128, 128], P(('rep', 'cplx'), 'row'), may hold values from -6 to 6
- residue_mask: int32 [16, 128], P(('rep', 'cplx')), may hold values from 0 to 1, as said below
- norm_outgo: float32 [128], replicated, may hold values from 0.25 to 1.75
- proj_outgo: bfloat16 [128, 640], replicated, may hold values from -0.5 to 0.5
- mid_outgo: float32 [128], replicated, may hold values from 0.25 to 1.75
- final_outgo: bfloat16 [128, 128], replicated, may hold values from -0.5 to 0.5
- norm_income: float32 [128], replicated, may hold values from 0.25 to 1.75
- proj_income: bfloat16 [128, 640], replicated, may hold values from -0.5 to 0.5
- mid_income: float32 [128], replicated, may hold values from 0.25 to 1.75
- final_income: bfloat16 [128, 128], replicated, may hold values from -0.5 to 0.5
Outputs:
- pair_grad: bfloat16 [16, 128, 128, 128], P(('rep', 'cplx'), 'row')
- norm_outgo_grad: float32 [128], replicated
- proj_outgo_grad: float32 [128, 640], replicated
- mid_outgo_grad: float32 [128], replicated
- final_outgo_grad: float32 [128, 128], replicated
- norm_income_grad: float32 [128], replicated
- proj_income_grad: float32 [128, 640], replicated
- mid_income_grad: float32 [128], replicated
- final_income_grad: float32 [128, 128], replicated
Inputs may be any that keep to these rules, and one draw needn't show every extreme that they name: `residue_mask`: each complex's mask is 1 on a prefix of at least 64 residues and 0 after it.
All inputs are finite; a program needn't handle non-finite values.
Results may differ from a plain program's by a relative error of at most 0.025.
Values may be sent and summed in bfloat16 or wider, within the bound.
A program may use at most 128 MiB of HBM per device.

v0:
```python
import math

import jax
import jax.numpy as jnp
from jax import lax
from jax.sharding import PartitionSpec as P

epsilon = 1e-05


def normalize(values):
    average = jnp.mean(values, -1, keepdims=True)
    centered = values - average
    inv_std = lax.rsqrt(jnp.mean(centered * centered, -1, keepdims=True) + epsilon)
    return (centered * inv_std, inv_std)


def norm_back(grad_hat, standard, inv_std):
    first = jnp.mean(grad_hat, -1, keepdims=True)
    second = jnp.mean(grad_hat * standard, -1, keepdims=True)
    return inv_std * (grad_hat - first - standard * second)


def matmul(left, right):
    flat = left.reshape(-1, left.shape[-1])
    result = jnp.dot(flat, right, preferred_element_type=jnp.float32)
    return result.reshape(left.shape[:-1] + (right.shape[-1],))


def contract(left, right):
    flat_left = left.reshape(-1, left.shape[-1])
    flat_right = right.reshape(-1, right.shape[-1])
    return jnp.dot(flat_left.T, flat_right, preferred_element_type=jnp.float32)


def front_part(block, row_mask, col_mask, norm_gain, projection):
    width = norm_gain.shape[0]
    hidden = (projection.shape[1] - width) // 4
    standard, inv_std = normalize(block.astype(jnp.float32))
    normed = (standard * norm_gain).astype(jnp.bfloat16)
    projected = matmul(normed, projection)
    pair_mask = (row_mask[:, None] * col_mask[None, :])[..., None]
    left = (
        jax.nn.sigmoid(projected[..., :hidden]) * projected[..., hidden : 2 * hidden] * pair_mask
    ).astype(jnp.bfloat16)
    right = (
        jax.nn.sigmoid(projected[..., 2 * hidden : 3 * hidden])
        * projected[..., 3 * hidden : 4 * hidden]
        * pair_mask
    ).astype(jnp.bfloat16)
    gate_value = jax.nn.sigmoid(projected[..., 4 * hidden :])
    return (left, right, (normed, standard, inv_std, projected, gate_value, pair_mask))


def finish(product, mid_gain, final):
    prod_hat, mid_inv = normalize(product)
    middle = (prod_hat * mid_gain).astype(jnp.bfloat16)
    update = matmul(middle, final)
    return (update, (prod_hat, mid_inv, middle, update))


def upper_back(upstream, saved, kept, mid_gain, final):
    gate_value = saved[4]
    prod_hat, mid_inv, middle, update = kept
    incoming = upstream.astype(jnp.float32)
    grad_update = (gate_value * incoming).astype(jnp.bfloat16)
    grad_gate = incoming * update * gate_value * (1.0 - gate_value)
    grad_middle = matmul(grad_update, final.T)
    final_grad = contract(middle, grad_update)
    mid_grad = jnp.sum((grad_middle * prod_hat).reshape(-1, prod_hat.shape[-1]), 0)
    grad_product = norm_back(grad_middle * mid_gain, prod_hat, mid_inv).astype(jnp.bfloat16)
    return (incoming, grad_gate, grad_product, final_grad, mid_grad)


def lower_back(incoming, grad_gate, grad_left, grad_right, saved, norm_gain, projection):
    normed, standard, inv_std, projected, gate_value, pair_mask = saved
    width = norm_gain.shape[0]
    hidden = (projection.shape[1] - width) // 4
    sig_left = jax.nn.sigmoid(projected[..., :hidden])
    sig_right = jax.nn.sigmoid(projected[..., 2 * hidden : 3 * hidden])
    grad_proj = jnp.concatenate(
        [
            grad_left
            * projected[..., hidden : 2 * hidden]
            * pair_mask
            * sig_left
            * (1.0 - sig_left),
            grad_left * sig_left * pair_mask,
            grad_right
            * projected[..., 3 * hidden : 4 * hidden]
            * pair_mask
            * sig_right
            * (1.0 - sig_right),
            grad_right * sig_right * pair_mask,
            grad_gate,
        ],
        -1,
    ).astype(jnp.bfloat16)
    proj_grad = contract(normed, grad_proj)
    grad_normed = matmul(grad_proj, projection.T)
    gain_grad = jnp.sum((grad_normed * standard).reshape(-1, width), 0)
    block_grad = (incoming + norm_back(grad_normed * norm_gain, standard, inv_std)).astype(
        jnp.bfloat16
    )
    return (block_grad, gain_grad, proj_grad)


def on_device(
    pair_map,
    cotangent,
    residue_mask,
    norm_outgo,
    proj_outgo,
    mid_outgo,
    final_outgo,
    norm_income,
    proj_income,
    mid_income,
    final_income,
):
    block = pair_map[0]
    upstream = cotangent[0]
    row_count = block.shape[0]
    length = block.shape[1]
    col_mask = residue_mask[0].astype(jnp.float32)
    row_mask = lax.dynamic_slice_in_dim(col_mask, lax.axis_index("row") * row_count, row_count, 0)
    left_one, right_one, saved_one = front_part(block, row_mask, col_mask, norm_outgo, proj_outgo)
    product_one = jnp.einsum(
        "ikc,jkc->ijc",
        left_one,
        lax.all_gather(right_one, "row", axis=0, tiled=True),
        preferred_element_type=jnp.float32,
    )
    update_one, kept_one = finish(product_one, mid_outgo, final_outgo)
    first_out = (block.astype(jnp.float32) + saved_one[4] * update_one).astype(jnp.bfloat16)
    left_two, right_two, saved_two = front_part(
        first_out, row_mask, col_mask, norm_income, proj_income
    )
    columns = left_two
    product_two = lax.psum_scatter(
        jnp.einsum("kic,kjc->ijc", columns, right_two, preferred_element_type=jnp.float32).astype(
            jnp.bfloat16
        ),
        "row",
        scatter_dimension=0,
        tiled=True,
    ).astype(jnp.float32)
    update_two, kept_two = finish(product_two, mid_income, final_income)
    incoming, grad_gate, grad_product, final_two, mid_two = upper_back(
        upstream, saved_two, kept_two, mid_income, final_income
    )
    piece = lax.all_gather(grad_product, "row", axis=0, tiled=True)
    left_part = jnp.einsum("ijc,kjc->kic", piece, right_two, preferred_element_type=jnp.float32)
    grad_left = left_part
    columns = left_two
    grad_right = jnp.einsum("kic,ijc->kjc", columns, piece, preferred_element_type=jnp.float32)
    grad_left, grad_right = (grad_left, grad_right)
    first_grad, gain_two, proj_two = lower_back(
        incoming, grad_gate, grad_left, grad_right, saved_two, norm_income, proj_income
    )
    incoming, grad_gate, grad_product, final_one, mid_one = upper_back(
        first_grad, saved_one, kept_one, mid_outgo, final_outgo
    )
    columns = grad_product
    grad_left = jnp.einsum(
        "ijc,jkc->ikc",
        columns,
        lax.all_gather(right_one, "row", axis=0, tiled=True),
        preferred_element_type=jnp.float32,
    )
    columns = grad_product
    grad_right = lax.psum_scatter(
        jnp.einsum("ijc,ikc->jkc", columns, left_one, preferred_element_type=jnp.float32).astype(
            jnp.bfloat16
        ),
        "row",
        scatter_dimension=0,
        tiled=True,
    ).astype(jnp.float32)
    block_grad, gain_one, proj_one = lower_back(
        incoming, grad_gate, grad_left, grad_right, saved_one, norm_outgo, proj_outgo
    )
    summed = lax.psum(
        (gain_one, proj_one, mid_one, final_one, gain_two, proj_two, mid_two, final_two),
        ("rep", "cplx", "row"),
    )
    factor = 1.0 / math.sqrt(lax.axis_size("rep") * lax.axis_size("cplx") * length * length)
    scaled = [item * factor for item in summed]
    return (
        block_grad[None],
        scaled[0],
        scaled[1],
        scaled[2],
        scaled[3],
        scaled[4],
        scaled[5],
        scaled[6],
        scaled[7],
    )


def solution(mesh):
    placed = (
        P(("rep", "cplx"), "row", None, None),
        P(("rep", "cplx"), "row", None, None),
        P(("rep", "cplx"), None),
        P(),
        P(),
        P(),
        P(),
        P(),
        P(),
        P(),
        P(),
    )
    return jax.shard_map(
        on_device,
        mesh=mesh,
        in_specs=placed,
        out_specs=(P(("rep", "cplx"), "row", None, None), P(), P(), P(), P(), P(), P(), P(), P()),
        check_vma=False,
    )
```

profile of v0, /device:TPU:1, one launch (start us, length us, event | category | flops | bytes accessed | tf_op | source)
XLA Modules:
  0.0 747.6 jit_solution(10212197812602243779)
XLA Ops:
  14.1 71.1 %all-gather.3.cloned.1.call-done = bf16[128,128,128]{2,1,0:T(8,128)(2,1)} async-done(((bf16[8,128,128]{2,1,0:T(8,128)(2,1)}), bf16[128,128,128]{2,1,0:T(8,128)(2,1)}) %all-gather.3.cloned.1.call-update) | async-done | bytes 4194320 | tf_op jit(solution)/shard_map/all_gather | solution.py:131
  85.2 6.6 copy.110
  91.8 4.5 fusion.133
  105.5 4.3 convert_bitcast_fusion.1
  109.8 7.3 copy.117
  117.2 76.5 %reduce-scatter.3.cloned.1.call-done = bf16[8,128,128]{2,1,0:T(8,128)(2,1)} async-done(((bf16[128,128,128]{2,1,0:T(8,128)(2,1)}), bf16[8,128,128]{2,1,0:T(8,128)(2,1)}) %reduce-scatter.3.cloned.1.call-update) | async-done | bytes 262160 | tf_op jit(solution)/shard_map/reduce_scatter | solution.py:140
  202.8 74.3 %all-gather.5.cloned.1.call-done = bf16[128,128,128]{2,1,0:T(8,128)(2,1)} async-done(((bf16[8,128,128]{2,1,0:T(8,128)(2,1)}), bf16[128,128,128]{2,1,0:T(8,128)(2,1)}) %all-gather.5.cloned.1.call-update) | async-done | bytes 4194320 | tf_op jit(solution)/shard_map/all_gather | solution.py:152
  277.2 6.7 copy.129
  283.9 4.4 fusion.135
  288.3 3.1 fusion.134
  291.4 2.1 copy.130
  293.5 2.0 copy.133
  304.1 3.3 fusion.137
  307.4 7.3 copy.142
  317.5 4.2 fusion.136
  322.9 3.1 convolution_bitcast_fusion.1
  326.0 2.0 convolution_bitcast_fusion.4
  328.9 2.1 fusion.98
  331.0 59.5 %reduce-scatter.5.cloned.1.call-done = bf16[8,128,128]{2,1,0:T(8,128)(2,1)} async-done(((bf16[128,128,128]{2,1,0:T(8,128)(2,1)}), bf16[8,128,128]{2,1,0:T(8,128)(2,1)}) %reduce-scatter.5.cloned.1.call-update) | async-done | bytes 262160 | tf_op jit(solution)/shard_map/reduce_scatter | solution.py:172
  390.5 2.0 fusion.103
  395.4 2.8 convolution_bitcast_fusion.2
  398.2 2.1 fusion.41
  400.3 84.7 %all-reduce = (f32[128]{0:T(128)S(1)}, f32[128]{0:T(128)S(1)}, f32[128]{0:T(128)S(1)}, f32[128]{0:T(128)S(1)}) all-reduce(f32[128]{0:T(128)S(1)} %get-tuple-element.15, f32[128]{0:T(128)S(1)} %get-tuple-element.9, f32[128]{0:T(128)S(1)} %get-tuple-element.13, ...), channel_id=1, replica_groups=mesh['rep'=4,'cplx'=4,'row'=16] {'rep','cplx','row'}, use_global_device_ids=true, to_apply=%region_19.0 | all-reduce | flops 512 | bytes 4096 | tf_op jit(solution)/shard_map/psum | solution.py:183
  488.4 246.3 %all-reduce.4.cloned.1.call-done = (f32[128,640]{1,0:T(8,128)}, f32[128,128]{1,0:T(8,128)}, f32[128,640]{1,0:T(8,128)}, f32[128,128]{1,0:T(8,128)}) async-done(((f32[128,640]{1,0:T(8,128)}, f32[128,128]{1,0:T(8,128)}, f32[128,640]{1,0:T(8,128)}, f32[128,128]{1,0:T(8,128)}), (f32[128,640]{1,0:T(8,128)}, f32[128,128]{1,0:T(8,128)}, f32[128,640]{1,0:T(8,128)}, ...) | async-done | bytes 786448 | tf_op jit(solution)/shard_map/psum | solution.py:183
  (131 shorter events, 51.2 us)
Async XLA Ops:
  7.2 91.4 %copy-start = (bf16[128,640]{1,0:T(8,128)(2,1)S(1)}, bf16[128,640]{1,0:T(8,128)(2,1)}, u32[]{:S(2)}) copy-start(bf16[128,640]{1,0:T(8,128)(2,1)} %param.19) | copy-start | bytes 491524
  7.2 78.0 %all-gather.3.cloned.1.call-start = ((), (), s32[]{:S(2)}) async-start(), calls=%async_computation.2 | async-start | bytes 4456448 | tf_op jit(solution)/shard_map/all_gather | solution.py:131
  13.2 180.5 %reduce-scatter.3.cloned.1.call-start = ((), (), s32[]{:S(2)}) async-start(), calls=%async_computation.3 | async-start | bytes 4456448 | tf_op jit(solution)/shard_map/reduce_scatter | solution.py:140
  91.8 4.7 copy-start.24
  91.8 4.9 copy-start.4
  91.8 4.9 copy-start.29
  96.8 3.9 copy-start.19
  117.1 80.4 %copy-start.27 = (f32[128]{0:T(128)S(1)}, f32[128]{0:T(128)}, u32[]{:S(2)}) copy-start(f32[128]{0:T(128)} %param.20) | copy-start | bytes 1540
  117.1 80.5 %copy-start.28 = (bf16[128,128]{1,0:T(8,128)(2,1)S(1)}, bf16[128,128]{1,0:T(8,128)(2,1)}, u32[]{:S(2)}) copy-start(bf16[128,128]{1,0:T(8,128)(2,1)} %param.21) | copy-start | bytes 98308
  117.1 160.1 %all-gather.5.cloned.1.call-start = ((), (), s32[]{:S(2)}) async-start(), calls=%async_computation.4 | async-start | bytes 4456448 | tf_op jit(solution)/shard_map/all_gather | solution.py:152
  202.6 187.9 %reduce-scatter.5.cloned.1.call-start = ((), (), s32[]{:S(2)}) async-start(), calls=%async_computation.5 | async-start | bytes 4456448 | tf_op jit(solution)/shard_map/reduce_scatter | solution.py:172
  283.9 4.4 copy-start.1
  283.9 4.4 copy-start.15
  295.5 3.3 copy-start.3
  295.5 3.3 copy-start.7
  301.5 2.6 copy-start.14
  314.7 2.8 copy-start.13
  314.7 420.0 %all-reduce.4.cloned.1.call-start = ((), (), s32[]{:S(2)}) async-start(), calls=%async_computation.6 | async-start | bytes 1572864 | tf_op jit(solution)/shard_map/psum | solution.py:183
  322.9 5.1 copy-start.6
  328.9 65.5 %copy-start.17 = (bf16[8,128,128]{2,1,0:T(8,128)(2,1)S(1)}, bf16[8,128,128]{2,1,0:T(8,128)(2,1)}, u32[]{:S(2)}) copy-start(bf16[8,128,128]{2,1,0:T(8,128)(2,1)} %copy-done.16) | copy-start | bytes 786436
  328.9 66.5 %copy-start.5 = (bf16[1,8,128,128]{3,2,1,0:T(8,128)(2,1)S(1)}, bf16[1,8,128,128]{3,2,1,0:T(8,128)(2,1)}, u32[]{:S(2)}) copy-start(bf16[1,8,128,128]{3,2,1,0:T(8,128)(2,1)} %param.11) | copy-start | bytes 786436
  328.9 66.5 %copy-start.26 = (f32[128]{0:T(128)S(1)}, f32[128]{0:T(128)}, u32[]{:S(2)}) copy-start(f32[128]{0:T(128)} %param.14) | copy-start | bytes 1540
  390.5 4.0 copy-start.21
  392.5 5.7 copy-start.23
  (11 other events, 16.1 us)
Sparse Core Ops, SparseCore 0:
  13.3 71.8 all-gather.2
  117.2 76.3 reduce-scatter.2
  202.7 74.4 all-gather.4
  314.8 75.6 reduce-scatter.4
  486.7 247.9 all-reduce.3
where the time goes:
time: 750 us; the launch traced here: 748 us
  waiting for transfers between devices  528 us (70%)
  blocking collectives  84.7 us (11%)
  local copies, waits for them, and re-layouts  44.9 us (6%)
  matrix products  41.8 us (6%)
  other arithmetic  33.6 us (4%)
  between operations  14.2 us (2%)
    psum x1, waiting for transfers between devices, on_device(): lax.psum((gain_one, proj_one, mid_one, final_one, gain_two, proj_two, mid...  246 us
    psum x1, blocking collectives, on_device(): lax.psum((gain_one, proj_one, mid_one, final_one, gain_two, proj_two, mid...  84.7 us
    reduce_scatter x1, waiting for transfers between devices, on_device(): lax.psum_scatter(jnp.einsum('kic,kjc->ijc', columns, right_two, preferred...  76.5 us
    all_gather x1, waiting for transfers between devices, on_device(): piece = lax.all_gather(grad_product, 'row', axis=0, tiled=True)  74.3 us
    all_gather x1, waiting for transfers between devices, on_device(): lax.all_gather(right_one, 'row', axis=0, tiled=True)  71.1 us
    reduce_scatter x1, waiting for transfers between devices, on_device(): lax.psum_scatter(jnp.einsum('ijc,ikc->jkc', columns, left_one, preferred_...  59.5 us
  transfers between devices with their start and end apart: 5, of which 5 were waited for; matrix products, arithmetic and copies ran while one was open for 2% of the time, Pallas kernels for 0%

commit v1 on v0

v1 whole, which is shorter than its diff:
```python
import functools
import math

import jax
import jax.numpy as jnp
from jax import lax
from jax.experimental import pallas as pl
from jax.experimental.pallas import tpu as pltpu
from jax.sharding import PartitionSpec as P

EPS = 1e-05
MESH = pl.DeviceIdType.MESH
F32 = jnp.float32
BF16 = jnp.bfloat16
ROWS = 16
TILE = 128
OWN = 8


def nn(a, b):
    return lax.dot_general(a, b, (((1,), (0,)), ((), ())), preferred_element_type=F32)


def nt(a, b):
    return lax.dot_general(a, b, (((1,), (1,)), ((), ())), preferred_element_type=F32)


def turn(a):
    return a.astype(F32).T.astype(BF16)


def tn(a, b):
    return nn(turn(a), b)


def mean0(a):
    return jnp.mean(a, axis=0, keepdims=True)


def normalize(a):
    centered = a - mean0(a)
    inv = lax.rsqrt(mean0(centered * centered) + EPS)
    return centered * inv, inv


def norm_back(e, standard, inv):
    return inv * (e - mean0(e) - standard * mean0(e * standard))


def kernel(
    groups, cplx_size, factor,
    pm, ct, mask, n1, w1, m1, f1, n2, w2, m2, f2,
    out, o_n1, o_p1, o_m1, o_f1, o_n2, o_p2, o_m2, o_f2,
    wt, ft, ngain, mgain, col, rowm,
    xt, std, inv, nrm, cf, gate, ph, minv, mdl, upd, gup, gproj, inc,
    s_a, s_b, ch_l, ch_r,
    gacc, macc, pay, vec,
    send2, recv2, send1, recv1,
    a2s, a2r, b2s, b2r, c2s, c2r, a1s, a1r, b1s, b1r, c1s, c1r,
    ssem, rsem,
):
    me = lax.axis_index("row")
    my_x, my_z = me // 8, lax.rem(me, 8)
    my_rep, my_cplx = lax.axis_index("rep"), lax.axis_index("cplx")
    mq = my_rep * cplx_size + my_cplx

    def row_to(t):
        return lax.rem(my_x + t // 8, 2) * 8 + lax.rem(my_z + lax.rem(t, 8), 8)

    def row_from(t):
        return lax.rem(my_x + 2 - t // 8, 2) * 8 + lax.rem(my_z + 8 - lax.rem(t, 8), 8)

    def grp_to(t):
        return lax.rem(mq + t, groups)

    def grp_from(t):
        return lax.rem(mq + groups - t, groups)

    def row_id(d):
        return {"row": d}

    def grp_id(d):
        return {"rep": d // cplx_size, "cplx": lax.rem(d, cplx_size)}

    barrier = pltpu.get_barrier_semaphore()

    def greet_row(t, _):
        pl.semaphore_signal(barrier, inc=1, device_id=row_id(row_to(t)), device_id_type=MESH)
        return 0

    def greet_grp(t, _):
        pl.semaphore_signal(barrier, inc=1, device_id=grp_id(grp_to(t)), device_id_type=MESH)
        return 0

    lax.fori_loop(1, ROWS, greet_row, 0)
    lax.fori_loop(1, groups, greet_grp, 0)

    def row_copy(src, dst, phase, d, slot):
        return pltpu.make_async_remote_copy(
            src_ref=src, dst_ref=dst, send_sem=ssem.at[phase, d], recv_sem=rsem.at[phase, slot],
            device_id=row_id(d), device_id_type=MESH)

    def grp_copy(src, dst, phase, d, slot):
        return pltpu.make_async_remote_copy(
            src_ref=src, dst_ref=dst, send_sem=ssem.at[phase, d], recv_sem=rsem.at[phase, slot],
            device_id=grp_id(d), device_id_type=MESH)

    def lanes(i):
        return pl.ds(pl.multiple_of(i * TILE, TILE), TILE)

    def tiles(body):
        def step(i, _):
            body(i)
            return 0

        lax.fori_loop(0, OWN, step, 0)

    def scatter(stages, send, recv, phase):
        def rows_of(d):
            return pl.ds(pl.multiple_of(d * 64, 64), 64)

        for n, stage in enumerate(stages):
            recv[me, n * 64 : n * 64 + 64, :] = stage[rows_of(me), :].astype(BF16)

        def body(t, _):
            d = row_to(t)
            for n, stage in enumerate(stages):
                send[d, n * 64 : n * 64 + 64, :] = stage[rows_of(d), :].astype(BF16)
            row_copy(send.at[d], recv.at[me], phase, d, me).start()
            return 0

        lax.fori_loop(1, ROWS, body, 0)

    def give_back(send, recv, phase):
        recv[me] = send[me]

        def body(t, _):
            d = row_to(t)
            row_copy(send.at[d], recv.at[me], phase, d, me).start()
            return 0

        lax.fori_loop(1, ROWS, body, 0)

    def settle(send, recv, phase, each=None):
        if each is not None:
            each(me)

        def body(t, _):
            s = row_from(t)
            row_copy(send.at[s], recv.at[s], phase, s, s).wait()
            if each is not None:
                each(s)
            return 0

        lax.fori_loop(1, ROWS, body, 0)

    def unstage(recv, stages):
        def each(s):
            for n, stage in enumerate(stages):
                stage[pl.ds(pl.multiple_of(s * 64, 64), 64), :] = recv[
                    s, n * 64 : n * 64 + 64, :
                ].astype(F32)

        return each

    def strided(i):
        return pl.ds(i, TILE, stride=OWN)

    def pair_of(recv, base, p):
        block = recv[:, pl.ds(pl.multiple_of(base + 16 * p, 16), 16), :].astype(F32)
        return [block[:, 8 * n : 8 * n + 8, :].reshape(TILE, TILE).astype(BF16) for n in range(2)]

    def put_pair(send, base, p, pair):
        both = jnp.concatenate([m.reshape(ROWS, 8, TILE) for m in pair], axis=1)
        send[:, pl.ds(pl.multiple_of(base + 16 * p, 16), 16), :] = both.astype(BF16)

    def pairs(body):
        def step(p, _):
            body(p)
            return 0

        lax.fori_loop(0, 4, step, 0)

    def forward_channels(u, recv, send):
        def body(p):
            left, right = pair_of(recv, 0, p), pair_of(recv, 64, p)
            result = []
            for n in range(2):
                ch_l[u, 2 * p + n] = left[n]
                ch_r[u, 2 * p + n] = right[n]
                result.append(nt(left[n], right[n]) if u == 0 else tn(left[n], right[n]))
            put_pair(send, 0, p, result)

        pairs(body)

    def backward_channels(u, recv, send):
        def body(p):
            grads = pair_of(recv, 0, p)
            lefts, rights = [], []
            for n in range(2):
                left, right, grad = ch_l[u, 2 * p + n], ch_r[u, 2 * p + n], grads[n]
                if u == 0:
                    lefts.append(nn(grad, right))
                    rights.append(tn(grad, left))
                else:
                    lefts.append(nt(right, grad))
                    rights.append(nn(left, grad))
            put_pair(send, 0, p, lefts)
            put_pair(send, 64, p, rights)

        pairs(body)

    def front(u, i, x):
        standard, inv_std = normalize(x)
        std[u, i] = standard
        inv[u, i] = inv_std
        normed = (standard * ngain[u]).astype(BF16)
        nrm[u, :, lanes(i)] = normed
        projected = nn(wt[u], normed)
        pair_mask = rowm[i] * col[...]
        s = jax.nn.sigmoid(projected[0:128])
        left = s * projected[128:256] * pair_mask
        cf[u, 0, i] = left * (1.0 - s)
        cf[u, 1, i] = s * pair_mask
        s_a[strided(i), :] = left
        t = jax.nn.sigmoid(projected[256:384])
        right = t * projected[384:512] * pair_mask
        cf[u, 2, i] = right * (1.0 - t)
        cf[u, 3, i] = t * pair_mask
        s_b[strided(i), :] = right
        gate[u, i] = jax.nn.sigmoid(projected[512:640])

    def finish(u, i):
        prod_hat, mid_inv = normalize(s_a[strided(i), :])
        middle = (prod_hat * mgain[u]).astype(BF16)
        update = nn(ft[u], middle)
        ph[u, i] = prod_hat
        minv[u, i] = mid_inv
        mdl[u, :, lanes(i)] = middle
        upd[u, i] = update
        return update, prod_hat, mid_inv

    def upper(u, i, incoming, update, prod_hat, mid_inv, final):
        g = gate[u, i]
        inc[u, i] = incoming
        grad_update = (g * incoming).astype(BF16)
        gup[u, :, lanes(i)] = grad_update
        gproj[u, 512:640, lanes(i)] = (incoming * update * g * (1.0 - g)).astype(BF16)
        grad_middle = nn(final[...], grad_update)
        macc[u] += grad_middle * prod_hat
        s_b[strided(i), :] = norm_back(grad_middle * mgain[u], prod_hat, mid_inv)

    def lower(u, i, weight):
        grad_left, grad_right = s_a[strided(i), :], s_b[strided(i), :]
        gproj[u, 0:128, lanes(i)] = (grad_left * cf[u, 0, i]).astype(BF16)
        gproj[u, 128:256, lanes(i)] = (grad_left * cf[u, 1, i]).astype(BF16)
        gproj[u, 256:384, lanes(i)] = (grad_right * cf[u, 2, i]).astype(BF16)
        gproj[u, 384:512, lanes(i)] = (grad_right * cf[u, 3, i]).astype(BF16)
        grad_normed = nn(weight[...], gproj[u, :, lanes(i)])
        standard = std[u, i]
        gacc[u] += grad_normed * standard
        back = norm_back(grad_normed * ngain[u], standard, inv[u, i])
        return (inc[u, i] + back).astype(BF16)

    for u, (w, f, n, m) in enumerate(((w1, f1, n1, m1), (w2, f2, n2, m2))):
        for g in range(5):
            wt[u, g * 128 : g * 128 + 128, :] = turn(w[:, g * 128 : g * 128 + 128])
        ft[u] = turn(f[...])
        ngain[u] = jnp.broadcast_to(n[...], (TILE, TILE)).T
        mgain[u] = jnp.broadcast_to(m[...], (TILE, TILE)).T
        gacc[u] = jnp.zeros((TILE, TILE), F32)
        macc[u] = jnp.zeros((TILE, TILE), F32)
    col_mask = mask[...].astype(F32)
    col[...] = col_mask
    where = lax.broadcasted_iota(jnp.int32, (1, TILE), 1)
    for i in range(OWN):
        picked = jnp.sum(jnp.where(where == me * OWN + i, col_mask, 0.0), axis=1, keepdims=True)
        rowm[i] = jnp.broadcast_to(picked, (1, TILE))

    def first(i):
        x = pm[0, i].astype(F32).T
        xt[i] = x
        front(0, i, x)

    tiles(first)
    pl.semaphore_wait(barrier, ROWS - 1 + groups - 1)
    scatter((s_a, s_b), send2.at[0], recv2.at[0], 0)
    settle(send2.at[0], recv2.at[0], 0)
    forward_channels(0, recv2.at[0], send1.at[0])
    give_back(send1.at[0], recv1.at[0], 1)
    settle(send1.at[0], recv1.at[0], 1, unstage(recv1.at[0], (s_a,)))

    def second(i):
        update, _, _ = finish(0, i)
        first_out = (xt[i] + gate[0, i] * update).astype(BF16)
        front(1, i, first_out.astype(F32))

    tiles(second)
    scatter((s_a, s_b), send2.at[1], recv2.at[1], 2)
    settle(send2.at[1], recv2.at[1], 2)
    forward_channels(1, recv2.at[1], send1.at[1])
    give_back(send1.at[1], recv1.at[1], 3)
    settle(send1.at[1], recv1.at[1], 3, unstage(recv1.at[1], (s_a,)))

    def third(i):
        update, prod_hat, mid_inv = finish(1, i)
        upper(1, i, ct[0, i].astype(F32).T, update, prod_hat, mid_inv, f2)

    tiles(third)
    scatter((s_b,), send1.at[2], recv1.at[2], 4)
    pay[640:768, :] = nt(mdl[1], gup[1])
    settle(send1.at[2], recv1.at[2], 4)
    backward_channels(1, recv1.at[2], send2.at[2])
    give_back(send2.at[2], recv2.at[2], 5)
    settle(send2.at[2], recv2.at[2], 5, unstage(recv2.at[2], (s_a, s_b)))

    def fourth(i):
        first_grad = lower(1, i, w2).astype(F32)
        upper(0, i, first_grad, upd[0, i], ph[0, i], minv[0, i], f1)

    tiles(fourth)
    scatter((s_b,), send1.at[3], recv1.at[3], 6)

    def vectors(values):
        vec[...] = jnp.zeros(vec.shape, F32)
        for n, value in enumerate(values):
            vec[n : n + 1, :] = jnp.sum(value.T, axis=0, keepdims=True)

    def blocks_out(send, recv, phase, block):
        def fill(d, ref):
            ref[d, 0:block, :] = pay[pl.ds(pl.multiple_of(d * block, block), block), :].astype(BF16)
            ref[d, block : block + 16, :] = vec[...].astype(BF16)

        fill(mq, recv)

        def body(t, _):
            d = grp_to(t)
            fill(d, send)
            grp_copy(send.at[d], recv.at[mq], phase, d, mq).start()
            return 0

        lax.fori_loop(1, groups, body, 0)

    def blocks_in(send, recv, phase):
        def body(t, _):
            s = grp_from(t)
            grp_copy(send.at[s], recv.at[s], phase, s, s).wait()
            return 0

        lax.fori_loop(1, groups, body, 0)
        return jnp.sum(recv[...].astype(F32), axis=0)

    def whole_out(value, send, recv, phase):
        send[...] = value.astype(BF16)
        recv[me] = value.astype(BF16)

        def body(t, _):
            d = row_to(t)
            row_copy(send, recv.at[me], phase, d, me).start()
            return 0

        lax.fori_loop(1, ROWS, body, 0)

    def whole_in(send, recv, phase):
        def body(t, _):
            s = row_from(t)
            row_copy(send, recv.at[s], phase, s, s).wait()
            return 0

        lax.fori_loop(1, ROWS, body, 0)
        return jnp.sum(recv[...].astype(F32), axis=0)

    def back_out(value, send, recv, phase):
        send[...] = value.astype(BF16)
        recv[mq] = value.astype(BF16)

        def body(t, _):
            d = grp_to(t)
            grp_copy(send, recv.at[mq], phase, d, mq).start()
            return 0

        lax.fori_loop(1, groups, body, 0)

    def back_in(send, recv, phase):
        def body(t, _):
            s = grp_from(t)
            grp_copy(send, recv.at[s], phase, s, s).wait()
            return 0

        lax.fori_loop(1, groups, body, 0)

    proj = nt(nrm[1], gproj[1])
    for g in range(5):
        pay[g * 128 : g * 128 + 128, :] = proj[:, g * 128 : g * 128 + 128]
    pay[768:896, :] = nt(mdl[0], gup[0])
    pay[896:1024, :] = nt(nrm[0], gproj[0, 512:640, :])
    vectors((gacc[1], macc[1], macc[0]))
    blocks_out(a2s, a2r, 8, 64)

    settle(send1.at[3], recv1.at[3], 6)
    backward_channels(0, recv1.at[3], send2.at[3])
    give_back(send2.at[3], recv2.at[3], 7)
    whole_out(blocks_in(a2s, a2r, 8), b2s, b2r, 9)
    settle(send2.at[3], recv2.at[3], 7, unstage(recv2.at[3], (s_a, s_b)))

    def fifth(i):
        out[0, i] = lower(0, i, w1).astype(F32).T.astype(BF16)

    tiles(fifth)
    proj = nt(nrm[0], gproj[0, 0:512, :])
    for g in range(4):
        pay[g * 128 : g * 128 + 128, :] = proj[:, g * 128 : g * 128 + 128]
    vectors((gacc[0],))
    blocks_out(a1s, a1r, 11, 32)

    total = whole_in(b2s, b2r, 9)
    back_out(total[0:64], c2s, c2r, 10)
    o_n2[...] = total[64:65] * factor
    o_m2[...] = total[65:66] * factor
    o_m1[...] = total[66:67] * factor

    whole_out(blocks_in(a1s, a1r, 11), b1s, b1r, 12)
    back_in(c2s, c2r, 10)
    sums = c2r[...].reshape(1024, TILE).astype(F32) * factor
    for g in range(5):
        o_p2[:, g * 128 : g * 128 + 128] = sums[g * 128 : g * 128 + 128]
    o_f2[...] = sums[640:768]
    o_f1[...] = sums[768:896]
    o_p1[:, 512:640] = sums[896:1024]

    total = whole_in(b1s, b1r, 12)
    back_out(total[0:32], c1s, c1r, 13)
    o_n1[...] = total[32:33] * factor
    back_in(c1s, c1r, 13)
    sums = c1r[...].reshape(512, TILE).astype(F32) * factor
    for g in range(4):
        o_p1[:, g * 128 : g * 128 + 128] = sums[g * 128 : g * 128 + 128]


def on_device(groups, cplx_size, factor, pm, ct, mask, n1, w1, m1, f1, n2, w2, m2, f2):
    wide = (1, TILE)
    shapes = [
        (pm.shape, BF16),
        (wide, F32), ((TILE, 640), F32), (wide, F32), ((TILE, TILE), F32),
        (wide, F32), ((TILE, 640), F32), (wide, F32), ((TILE, TILE), F32),
    ]
    tile = (OWN, TILE, TILE)
    lane = (TILE, OWN * TILE)
    scratch = [
        pltpu.VMEM((2, 640, TILE), BF16),
        pltpu.VMEM((2, TILE, TILE), BF16),
        pltpu.VMEM((2, TILE, TILE), F32),
        pltpu.VMEM((2, TILE, TILE), F32),
        pltpu.VMEM(wide, F32),
        pltpu.VMEM((OWN, 1, TILE), F32),
        pltpu.VMEM(tile, F32),
        pltpu.VMEM((2,) + tile, F32),
        pltpu.VMEM((2, OWN, 1, TILE), F32),
        pltpu.VMEM((2,) + lane, BF16),
        pltpu.VMEM((2, 4) + tile, F32),
        pltpu.VMEM((2,) + tile, F32),
        pltpu.VMEM((2,) + tile, F32),
        pltpu.VMEM((2, OWN, 1, TILE), F32),
        pltpu.VMEM((2,) + lane, BF16),
        pltpu.VMEM((2,) + tile, F32),
        pltpu.VMEM((2,) + lane, BF16),
        pltpu.VMEM((2, 640, OWN * TILE), BF16),
        pltpu.VMEM((2,) + tile, F32),
        pltpu.VMEM((OWN * TILE, TILE), F32),
        pltpu.VMEM((OWN * TILE, TILE), F32),
        pltpu.VMEM((2,) + tile, BF16),
        pltpu.VMEM((2,) + tile, BF16),
        pltpu.VMEM((2, TILE, TILE), F32),
        pltpu.VMEM((2, TILE, TILE), F32),
        pltpu.VMEM((1024, TILE), F32),
        pltpu.VMEM((16, TILE), F32),
        pltpu.VMEM((4, ROWS, 128, TILE), BF16),
        pltpu.VMEM((4, ROWS, 128, TILE), BF16),
        pltpu.VMEM((4, ROWS, 64, TILE), BF16),
        pltpu.VMEM((4, ROWS, 64, TILE), BF16),
        pltpu.VMEM((16, 80, TILE), BF16),
        pltpu.VMEM((16, 80, TILE), BF16),
        pltpu.VMEM((80, TILE), BF16),
        pltpu.VMEM((ROWS, 80, TILE), BF16),
        pltpu.VMEM((64, TILE), BF16),
        pltpu.VMEM((16, 64, TILE), BF16),
        pltpu.VMEM((16, 48, TILE), BF16),
        pltpu.VMEM((16, 48, TILE), BF16),
        pltpu.VMEM((48, TILE), BF16),
        pltpu.VMEM((ROWS, 48, TILE), BF16),
        pltpu.VMEM((32, TILE), BF16),
        pltpu.VMEM((16, 32, TILE), BF16),
        pltpu.SemaphoreType.DMA((14, 16)),
        pltpu.SemaphoreType.DMA((14, 16)),
    ]
    vmem = pl.BlockSpec(memory_space=pltpu.VMEM)
    results = pl.pallas_call(
        functools.partial(kernel, groups, cplx_size, factor),
        out_shape=[jax.ShapeDtypeStruct(s, d) for s, d in shapes],
        in_specs=[vmem] * 11,
        out_specs=[vmem] * 9,
        scratch_shapes=scratch,
        compiler_params=pltpu.CompilerParams(
            collective_id=0, has_side_effects=True, vmem_limit_bytes=48 * 1024 * 1024
        ),
        name="triangle",
    )(
        pm, ct, mask,
        n1.reshape(wide), w1, m1.reshape(wide), f1,
        n2.reshape(wide), w2, m2.reshape(wide), f2,
    )
    flat = [r.reshape(TILE) if r.shape == wide else r for r in results]
    return tuple(flat)


def solution(mesh):
    groups = mesh.shape["rep"] * mesh.shape["cplx"]
    factor = 1.0 / math.sqrt(groups * TILE * TILE)
    blocks = P(("rep", "cplx"), "row", None, None)
    placed = (blocks, blocks, P(("rep", "cplx"), None)) + (P(),) * 8
    return jax.shard_map(
        functools.partial(on_device, groups, mesh.shape["cplx"], factor),
        mesh=mesh,
        in_specs=placed,
        out_specs=(blocks,) + (P(),) * 8,
        check_vma=False,
    )
```

time: 750 us -> 155 us (0.21)
  waiting for transfers between devices: 528 us -> 0 us
  Pallas kernels: 0 us -> 143 us
  blocking collectives: 84.7 us -> 0 us
  matrix products: 41.8 us -> 0 us
  other arithmetic: 33.6 us -> 0 us
  local copies, waits for them, and re-layouts: 44.9 us -> 11.4 us
  between operations: 14.2 us -> 0.71 us
    psum x1 -> x0, waiting for transfers between devices: 246 us -> none  [on_device(): lax.psum((gain_one, proj_one, mid_one, final_one, gain_two, proj_two, mid...]
    all_gather x2 -> x0, waiting for transfers between devices: 145 us -> none  [the longest x1 74.3 us: on_device(): piece = lax.all_gather(grad_product, 'row', axis=0, tiled=True)]
    pallas_call x0 -> x1, Pallas kernels: none -> 143 us  [on_device(): pl.pallas_call(functools.partial(kernel, groups, cplx_size, factor), out_...]
    reduce_scatter x2 -> x0, waiting for transfers between devices: 136 us -> none  [the longest x1 76.5 us: on_device(): lax.psum_scatter(jnp.einsum('kic,kjc->ijc', columns, right_two, preferred...]
    psum x1 -> x0, blocking collectives: 84.7 us -> none  [on_device(): lax.psum((gain_one, proj_one, mid_one, final_one, gain_two, proj_two, mid...]
    dot_general x18 -> x0, matrix products: 41.8 us -> none  [the longest x4 9.71 us: contract(): return jnp.dot(flat_left.T, flat_right, preferred_element_type=jnp.float32)]
    convert_element_type x5 -> x0, local copies, waits for them, and re-layouts: 13.6 us -> none  [the longest x1 7.27 us: on_device(): jnp.einsum('kic,kjc->ijc', columns, right_two, preferred_element_type=jnp...]
    all_gather x2 -> x0, local copies, waits for them, and re-layouts: 13.4 us -> none  [the longest x1 6.72 us: on_device(): piece = lax.all_gather(grad_product, 'row', axis=0, tiled=True)]
  transfers between devices with their start and end apart: 5 -> 0, of which waited for: 5 -> 0; matrix products, arithmetic and copies ran while one was open for 2% -> 0% of each run, Pallas kernels for 0% -> 0%
where the time goes in v1:
time: 155 us
  Pallas kernels  143 us (92%)
  local copies, waits for them, and re-layouts  11.4 us (7%)
    pallas_call x1, Pallas kernels, on_device(): pl.pallas_call(functools.partial(kernel, groups, cplx_size, factor), out_...  143 us
    unnamed x31, local copies, waits for them, and re-layouts  11.4 us

profile of v1, /device:TPU:1, one launch (start us, length us, event | category | flops | bytes accessed | tf_op | source)
XLA Modules:
  0.0 154.8 jit_solution(7407696691700629461)
XLA Ops:
  0.6 0.0 copy-start.9
  0.7 0.0 copy-start.10
  0.7 0.0 copy-start.6
  0.7 0.6 copy-done.9
  1.3 0.0 copy-done.10
  1.3 0.0 copy-done.6
  1.3 0.0 copy-done.7
  1.4 0.0 copy-done.8
  1.4 0.9 copy-done
  2.3 0.9 copy-done.1
  3.3 0.9 copy-done.2
  4.2 0.9 copy-done.3
  5.1 0.8 copy-done.4
  5.9 0.8 copy-done.5
  6.6 142.7 %triangle.1 = (bf16[1,8,128,128]{3,2,1,0:T(8,128)(2,1)S(1)}, f32[1,128]{1,0:T(1,128)S(1)}, f32[128,640]{1,0:T(8,128)S(1)}, f32[1,128]{1,0:T(1,128)S(1)}, f32[128...) custom-call(bf16[1,8,128,128]{3,2,1,0:T(8,128)(2,1)S(1)} %copy-done,, ...), custom_call_target="tpu_custom_call" | custom-call | tf_op jit(solution)/shard_map/triangle/pallas_call | solution.py:497
  149.4 0.7 copy.29
  150.1 0.5 copy.30
  150.6 0.7 copy.31
  151.3 0.5 copy.32
  151.8 0.6 copy.33
  152.5 0.5 copy.34
  153.0 0.7 copy.35
  153.7 0.5 copy.36
  154.2 0.6 copy.37
  (8 shorter events, 0.0 us)
Async XLA Ops:
  0.6 0.7 copy-start.9
  0.7 0.7 copy-start.10
  0.7 0.7 copy-start.6
  0.7 0.7 copy-start.7
  0.7 0.7 copy-start.8
  1.4 0.9 copy-start
  2.3 0.9 copy-start.1
  3.3 0.9 copy-start.2
  4.2 0.9 copy-start.3
  5.1 0.8 copy-start.4
  5.9 0.8 copy-start.5

commit v2 on v1

--- a/solution.py
+++ b/solution.py
@@ -14,6 +14,7 @@
 BF16 = jnp.bfloat16
 ROWS = 16
 TILE = 128
+VMEM_BYTES = 63 * 1024 * 1024
 OWN = 8
 
 
@@ -49,6 +50,8 @@
 
 def kernel(
     groups, cplx_size, factor,
+    pm_in, ct_in, mask_in, n1_in, w1_in, m1_in, f1_in, n2_in, w2_in, m2_in, f2_in,
+    out_to, n1_to, p1_to, m1_to, f1_to, n2_to, p2_to, m2_to, f2_to,
     pm, ct, mask, n1, w1, m1, f1, n2, w2, m2, f2,
     out, o_n1, o_p1, o_m1, o_f1, o_n2, o_p2, o_m2, o_f2,
     wt, ft, ngain, mgain, col, rowm,
@@ -57,18 +60,24 @@
     gacc, macc, pay, vec,
     send2, recv2, send1, recv1,
     a2s, a2r, b2s, b2r, c2s, c2r, a1s, a1r, b1s, b1r, c1s, c1r,
-    ssem, rsem,
+    ssem, rsem, isem, osem,
 ):
     me = lax.axis_index("row")
     my_x, my_z = me // 8, lax.rem(me, 8)
     my_rep, my_cplx = lax.axis_index("rep"), lax.axis_index("cplx")
     mq = my_rep * cplx_size + my_cplx
 
+    def offsets(t):
+        n = lax.rem(t - 1, 8)
+        return 1 - (t - 1) // 8, lax.rem(12 + (2 * lax.rem(n, 2) - 1) * ((n + 1) // 2), 8)
+
     def row_to(t):
-        return lax.rem(my_x + t // 8, 2) * 8 + lax.rem(my_z + lax.rem(t, 8), 8)
+        dx, dz = offsets(t)
+        return lax.rem(my_x + dx, 2) * 8 + lax.rem(my_z + dz, 8)
 
     def row_from(t):
-        return lax.rem(my_x + 2 - t // 8, 2) * 8 + lax.rem(my_z + 8 - lax.rem(t, 8), 8)
+        dx, dz = offsets(t)
+        return lax.rem(my_x + dx, 2) * 8 + lax.rem(my_z + 8 - dz, 8)
 
     def grp_to(t):
         return lax.rem(mq + t, groups)
@@ -92,6 +101,16 @@
         pl.semaphore_signal(barrier, inc=1, device_id=grp_id(grp_to(t)), device_id_type=MESH)
         return 0
 
+    loads = [
+        pltpu.make_async_copy(a, b, isem.at[n])
+        for n, (a, b) in enumerate((
+            (pm_in, pm), (w1_in, w1), (n1_in, n1), (mask_in, mask),
+            (f1_in, f1), (m1_in, m1), (w2_in, w2), (n2_in, n2),
+            (f2_in, f2), (m2_in, m2), (ct_in, ct),
+        ))
+    ]
+    for load in loads:
+        load.start()
     lax.fori_loop(1, ROWS, greet_row, 0)
     lax.fori_loop(1, groups, greet_grp, 0)
 
@@ -113,7 +132,7 @@
             body(i)
             return 0
 
-        lax.fori_loop(0, OWN, step, 0)
+        lax.fori_loop(0, OWN, step, 0, unroll=4)
 
     def scatter(stages, send, recv, phase):
         def rows_of(d):
@@ -179,7 +198,7 @@
             body(p)
             return 0
 
-        lax.fori_loop(0, 4, step, 0)
+        lax.fori_loop(0, 4, step, 0, unroll=2)
 
     def forward_channels(u, recv, send):
         def body(p):
@@ -262,14 +281,17 @@
         back = norm_back(grad_normed * ngain[u], standard, inv[u, i])
         return (inc[u, i] + back).astype(BF16)
 
-    for u, (w, f, n, m) in enumerate(((w1, f1, n1, m1), (w2, f2, n2, m2))):
+    def spread(row):
+        return jnp.broadcast_to(row[...], (TILE, TILE)).T
+
+    def weights(u, w, n):
         for g in range(5):
             wt[u, g * 128 : g * 128 + 128, :] = turn(w[:, g * 128 : g * 128 + 128])
-        ft[u] = turn(f[...])
-        ngain[u] = jnp.broadcast_to(n[...], (TILE, TILE)).T
-        mgain[u] = jnp.broadcast_to(m[...], (TILE, TILE)).T
-        gacc[u] = jnp.zeros((TILE, TILE), F32)
-        macc[u] = jnp.zeros((TILE, TILE), F32)
+        ngain[u] = spread(n)
+
+    for load in loads[0:4]:
+        load.wait()
+    weights(0, w1, n1)
     col_mask = mask[...].astype(F32)
     col[...] = col_mask
     where = lax.broadcasted_iota(jnp.int32, (1, TILE), 1)
@@ -285,6 +307,14 @@
     tiles(first)
     pl.semaphore_wait(barrier, ROWS - 1 + groups - 1)
     scatter((s_a, s_b), send2.at[0], recv2.at[0], 0)
+    for load in loads[4:]:
+        load.wait()
+    weights(1, w2, n2)
+    for u, (f, m) in enumerate(((f1, m1), (f2, m2))):
+        ft[u] = turn(f[...])
+        mgain[u] = spread(m)
+        gacc[u] = jnp.zeros((TILE, TILE), F32)
+        macc[u] = jnp.zeros((TILE, TILE), F32)
     settle(send2.at[0], recv2.at[0], 0)
     forward_channels(0, recv2.at[0], send1.at[0])
     give_back(send1.at[0], recv1.at[0], 1)
@@ -407,6 +437,13 @@
         out[0, i] = lower(0, i, w1).astype(F32).T.astype(BF16)
 
     tiles(fifth)
+    stores = [pltpu.make_async_copy(out, out_to, osem.at[0])]
+    stores[0].start()
+
+    def store(n, a, b):
+        stores.append(pltpu.make_async_copy(a, b, osem.at[n]))
+        stores[-1].start()
+
     proj = nt(nrm[0], gproj[0, 0:512, :])
     for g in range(4):
         pay[g * 128 : g * 128 + 128, :] = proj[:, g * 128 : g * 128 + 128]
@@ -418,6 +455,9 @@
     o_n2[...] = total[64:65] * factor
     o_m2[...] = total[65:66] * factor
     o_m1[...] = total[66:67] * factor
+    store(1, o_n2, n2_to)
+    store(2, o_m2, m2_to)
+    store(3, o_m1, m1_to)
 
     whole_out(blocks_in(a1s, a1r, 11), b1s, b1r, 12)
     back_in(c2s, c2r, 10)
@@ -427,14 +467,35 @@
     o_f2[...] = sums[640:768]
     o_f1[...] = sums[768:896]
     o_p1[:, 512:640] = sums[896:1024]
+    store(4, o_p2, p2_to)
+    store(5, o_f2, f2_to)
+    store(6, o_f1, f1_to)
 
     total = whole_in(b1s, b1r, 12)
     back_out(total[0:32], c1s, c1r, 13)
     o_n1[...] = total[32:33] * factor
+    store(7, o_n1, n1_to)
     back_in(c1s, c1r, 13)
     sums = c1r[...].reshape(512, TILE).astype(F32) * factor
     for g in range(4):
         o_p1[:, g * 128 : g * 128 + 128] = sums[g * 128 : g * 128 + 128]
+
+    store(8, o_p1, p1_to)
+    for copy in stores:
+        copy.wait()
+
+
+def hand_on(*refs):
+    froms, tos, held, sems = refs[:9], refs[9:18], refs[18:27], refs[27]
+    loads = [pltpu.make_async_copy(a, b, sems.at[0, n]) for n, (a, b) in enumerate(zip(froms, held))]
+    stores = [pltpu.make_async_copy(a, b, sems.at[1, n]) for n, (a, b) in enumerate(zip(held, tos))]
+    for load in loads:
+        load.start()
+    for load, store in zip(loads, stores):
+        load.wait()
+        store.start()
+    for store in stores:
+        store.wait()
 
 
 def on_device(groups, cplx_size, factor, pm, ct, mask, n1, w1, m1, f1, n2, w2, m2, f2):
@@ -446,7 +507,12 @@
     ]
     tile = (OWN, TILE, TILE)
     lane = (TILE, OWN * TILE)
-    scratch = [
+    loaded = [
+        (pm.shape, BF16), (ct.shape, BF16), (mask.shape, jnp.int32),
+        (wide, F32), ((TILE, 640), BF16), (wide, F32), ((TILE, TILE), BF16),
+        (wide, F32), ((TILE, 640), BF16), (wide, F32), ((TILE, TILE), BF16),
+    ]
+    scratch = [pltpu.VMEM(s, d) for s, d in loaded + shapes] + [
         pltpu.VMEM((2, 640, TILE), BF16),
         pltpu.VMEM((2, TILE, TILE), BF16),
         pltpu.VMEM((2, TILE, TILE), F32),
@@ -492,16 +558,18 @@
         pltpu.VMEM((16, 32, TILE), BF16),
         pltpu.SemaphoreType.DMA((14, 16)),
         pltpu.SemaphoreType.DMA((14, 16)),
+        pltpu.SemaphoreType.DMA((11,)),
+        pltpu.SemaphoreType.DMA((9,)),
     ]
-    vmem = pl.BlockSpec(memory_space=pltpu.VMEM)
+    anywhere = pl.BlockSpec(memory_space=pl.ANY)
     results = pl.pallas_call(
         functools.partial(kernel, groups, cplx_size, factor),
         out_shape=[jax.ShapeDtypeStruct(s, d) for s, d in shapes],
-        in_specs=[vmem] * 11,
-        out_specs=[vmem] * 9,
+        in_specs=[anywhere] * 11,
+        out_specs=[anywhere] * 9,
         scratch_shapes=scratch,
         compiler_params=pltpu.CompilerParams(
-            collective_id=0, has_side_effects=True, vmem_limit_bytes=48 * 1024 * 1024
+            collective_id=0, has_side_effects=True, vmem_limit_bytes=VMEM_BYTES
         ),
         name="triangle",
     )(
@@ -509,6 +577,15 @@
         n1.reshape(wide), w1, m1.reshape(wide), f1,
         n2.reshape(wide), w2, m2.reshape(wide), f2,
     )
+    results = pl.pallas_call(
+        hand_on,
+        out_shape=[jax.ShapeDtypeStruct(s, d) for s, d in shapes],
+        in_specs=[anywhere] * 9,
+        out_specs=[anywhere] * 9,
+        scratch_shapes=[pltpu.VMEM(s, d) for s, d in shapes] + [pltpu.SemaphoreType.DMA((2, 9))],
+        compiler_params=pltpu.CompilerParams(vmem_limit_bytes=VMEM_BYTES),
+        name="hand_on",
+    )(*results)
     flat = [r.reshape(TILE) if r.shape == wide else r for r in results]
     return tuple(flat)
 

time: 155 us -> 132 us (0.85)
  Pallas kernels: 143 us -> 131 us
  local copies, waits for them, and re-layouts: 11.4 us -> 0 us
    pallas_call x1, Pallas kernels: 143 us -> 129 us  [on_device(): pl.pallas_call(functools.partial(kernel, groups, cplx_size, factor), out_...]
    unnamed x31 -> x0, local copies, waits for them, and re-layouts: 11.4 us -> none
    pallas_call x0 -> x1, Pallas kernels: none -> 2.1 us  [on_device(): pl.pallas_call(hand_on, out_shape=[jax.ShapeDtypeStruct(s, d) for s, d in...]
where the time goes in v2:
time: 132 us
  Pallas kernels  131 us (99%)
    pallas_call x1, Pallas kernels, on_device(): pl.pallas_call(functools.partial(kernel, groups, cplx_size, factor), out_...  129 us

profile of v2, /device:TPU:1, one launch (start us, length us, event | category | flops | bytes accessed | tf_op | source)
XLA Modules:
  0.0 131.9 jit_solution(11404559986073362330)
XLA Ops:
  0.6 129.2 %triangle.1 = (bf16[1,8,128,128]{3,2,1,0:T(8,128)(2,1)}, f32[1,128]{1,0:T(1,128)}, f32[128,640]{1,0:T(8,128)}, f32[1,128]{1,0:T(1,128)}, f32[128,128]{1,0:T(8,12...) custom-call(bf16[1,8,128,128]{3,2,1,0:T(8,128)(2,1)} %pm_in.1, ...), custom_call_target="tpu_custom_call" | custom-call | tf_op jit(solution)/shard_map/triangle/pallas_call | solution.py:565
  129.8 2.1 %hand_on.1 = (bf16[1,8,128,128]{3,2,1,0:T(8,128)(2,1)}, f32[1,128]{1,0:T(1,128)}, f32[128,640]{1,0:T(8,128)}, f32[1,128]{1,0:T(1,128)}, f32[128,128]{1,0:T(8,128...) custom-call(bf16[1,8,128,128]{3,2,1,0:T(8,128)(2,1)} %get-tuple-element.27.refs_0_, ...), custom_call_target="tpu_custom_call" | custom-call | tf_op jit(solution)/shard_map/hand_on/pallas_call | solution.py:580

commit v3 on v2

v3 whole, which is shorter than its diff:
```python
import functools
import math

import jax
import jax.numpy as jnp
from jax import lax
from jax.experimental import pallas as pl
from jax.experimental.pallas import tpu as pltpu
from jax.sharding import PartitionSpec as P

EPS = 1e-05
MESH = pl.DeviceIdType.MESH
F32 = jnp.float32
BF16 = jnp.bfloat16
ROWS = 16
TILE = 128
VMEM_BYTES = 63 * 1024 * 1024
OWN = 8
PART = 4


def nn(a, b):
    return lax.dot_general(a, b, (((1,), (0,)), ((), ())), preferred_element_type=F32)


def nt(a, b):
    return lax.dot_general(a, b, (((1,), (1,)), ((), ())), preferred_element_type=F32)


def turn(a):
    return a.astype(F32).T.astype(BF16)


def tn(a, b):
    return nn(turn(a), b)


def mean0(a):
    return jnp.mean(a, axis=0, keepdims=True)


def normalize(a):
    centered = a - mean0(a)
    inv = lax.rsqrt(mean0(centered * centered) + EPS)
    return centered * inv, inv


def norm_back(e, standard, inv):
    return inv * (e - mean0(e) - standard * mean0(e * standard))


def kernel(
    groups, factor,
    pm_in, ct_in, mask_in, n1_in, w1_in, m1_in, f1_in, n2_in, w2_in, m2_in, f2_in,
    out_to, n1_to, p1_to, m1_to, f1_to, n2_to, p2_to, m2_to, f2_to,
    pm, ct, masks, n1, w1, m1, f1, n2, w2, m2, f2,
    out, o_n1, o_p1, o_m1, o_f1, o_n2, o_p2, o_m2, o_f2,
    wt, ft, ngain, mgain, rowm,
    xt, std, inv, nrm, cf, gate, ph, minv, mdl, upd, gup, gproj, inc,
    s_a, s_b, ch_l, ch_r,
    gacc, macc, pay, vec,
    send2, recv2, send1, recv1,
    a2s, a2r, b2s, b2r, c2s, c2r, a1s, a1r, b1s, b1r, c1s, c1r,
    ssem, rsem, isem, osem, xsem, ysem,
):
    me = lax.axis_index("row")
    my_x, my_z = me // 8, lax.rem(me, 8)
    my_rep, my_cplx = lax.axis_index("rep"), lax.axis_index("cplx")
    side, core = my_rep // 2, lax.rem(my_rep, 2)
    mate = 1 - core
    mq = my_rep * 4 + my_cplx

    def offsets(t):
        n = lax.rem(t - 1, 8)
        return 1 - (t - 1) // 8, lax.rem(12 + (2 * lax.rem(n, 2) - 1) * ((n + 1) // 2), 8)

    def row_to(t):
        dx, dz = offsets(t)
        return lax.rem(my_x + dx, 2) * 8 + lax.rem(my_z + dz, 8)

    def row_from(t):
        dx, dz = offsets(t)
        return lax.rem(my_x + dx, 2) * 8 + lax.rem(my_z + 8 - dz, 8)

    def grp_offsets(t):
        a, n = 3 - (t - 1) // 4, lax.rem(t - 1, 4)
        return a, lax.rem(6 + (2 * lax.rem(n, 2) - 1) * ((n + 1) // 2), 4)

    def grp_at(a, dy):
        r = lax.rem(side + a // 2, 2) * 2 + lax.rem(core + lax.rem(a, 2), 2)
        return r * 4 + lax.rem(my_cplx + dy, 4)

    def grp_to(t):
        a, dy = grp_offsets(t)
        return grp_at(a, dy)

    def grp_from(t):
        a, dy = grp_offsets(t)
        return grp_at(a, 4 - dy)

    def row_id(d, h):
        return {"rep": side * 2 + h, "row": d}

    def grp_id(d):
        return {"rep": d // 4, "cplx": lax.rem(d, 4)}

    barrier = pltpu.get_barrier_semaphore()

    def greet_row(t, _):
        for h in range(2):
            pl.semaphore_signal(barrier, inc=1, device_id=row_id(row_to(t), h), device_id_type=MESH)
        return 0

    def greet_grp(t, _):
        pl.semaphore_signal(barrier, inc=1, device_id=grp_id(grp_to(t)), device_id_type=MESH)
        return 0

    mine, theirs = pl.ds(core * PART, PART), pl.ds(mate * PART, PART)
    loads = [
        pltpu.make_async_copy(a, b, isem.at[n])
        for n, (a, b) in enumerate((
            (pm_in.at[0, mine], pm.at[mine]), (w1_in, w1), (n1_in, n1), (mask_in, masks.at[core]),
            (f1_in, f1), (m1_in, m1), (w2_in, w2), (n2_in, n2),
            (f2_in, f2), (m2_in, m2), (ct_in.at[0, mine], ct.at[mine]),
        ))
    ]
    for load in loads:
        load.start()
    lax.fori_loop(1, ROWS, greet_row, 0)
    lax.fori_loop(1, groups, greet_grp, 0)

    def swap(n, src, dst):
        return pltpu.make_async_remote_copy(
            src_ref=src, dst_ref=dst, send_sem=xsem.at[n], recv_sem=ysem.at[n],
            device_id=row_id(me, mate), device_id_type=MESH)

    def row_copy(src, dst, phase, d, h, n, slot):
        return pltpu.make_async_remote_copy(
            src_ref=src, dst_ref=dst, send_sem=ssem.at[phase, n], recv_sem=rsem.at[phase, slot],
            device_id=row_id(d, h), device_id_type=MESH)

    def grp_copy(src, dst, phase, d, slot):
        return pltpu.make_async_remote_copy(
            src_ref=src, dst_ref=dst, send_sem=ssem.at[phase, d], recv_sem=rsem.at[phase, slot],
            device_id=grp_id(d), device_id_type=MESH)

    def lanes(i):
        return pl.ds(pl.multiple_of(i * TILE, TILE), TILE)

    def tiles(chain, body):
        def step(i, _):
            body(chain * PART + i, chain, i)
            return 0

        lax.fori_loop(0, PART, step, 0, unroll=4)

    def scatter(chain, stages, send, recv, phase):
        def fill(d, slot, ref):
            for n, stage in enumerate(stages):
                ref[slot, n * 32 : n * 32 + 32, :] = stage[
                    chain, pl.ds(pl.multiple_of(d * 32, 32), 32), :
                ].astype(BF16)

        def post(d):
            slot = chain * ROWS + d
            fill(d, slot, send)
            row_copy(send.at[slot], recv.at[core * ROWS + me], phase, d, chain, slot,
                     core * ROWS + me).start()

        def body(t, _):
            post(row_to(t))
            return 0

        lax.fori_loop(1, ROWS, body, 0)

        @pl.when(core == chain)
        def _():
            fill(me, core * ROWS + me, recv)

        @pl.when(core != chain)
        def _():
            post(me)

    def others(body):
        def step(t, _):
            d = row_to(t)
            body(d, 0)
            body(d, 1)
            return 0

        lax.fori_loop(1, ROWS, step, 0)
        body(me, mate)

    def give_back(send, recv, phase):
        def post(d, h):
            slot = h * ROWS + d
            row_copy(send.at[slot], recv.at[core * ROWS + me], phase, d, h, slot,
                     core * ROWS + me).start()

        others(post)
        recv[core * ROWS + me] = send[core * ROWS + me]

    def others_from(body):
        def step(t, _):
            s = row_from(t)
            body(s, 0)
            body(s, 1)
            return 0

        lax.fori_loop(1, ROWS, step, 0)
        body(me, mate)

    def gathered(recv, phase):
        def take(s, h):
            slot = h * ROWS + s
            row_copy(recv.at[slot], recv.at[slot], phase, s, h, slot, slot).wait_recv()

        others_from(take)

    def returned(chain, recv, phase, stages):
        def take(s):
            slot = chain * ROWS + s
            for n, stage in enumerate(stages):
                stage[chain, pl.ds(pl.multiple_of(s * 32, 32), 32), :] = recv[
                    slot, n * 32 : n * 32 + 32, :
                ].astype(F32)

        def wait(s):
            slot = chain * ROWS + s
            row_copy(recv.at[slot], recv.at[slot], phase, s, chain, slot, slot).wait_recv()

        @pl.when(core != chain)
        def _():
            wait(me)

        take(me)

        def body(t, _):
            s = row_from(t)
            wait(s)
            take(s)
            return 0

        lax.fori_loop(1, ROWS, body, 0)

    def sent(send, phase):
        def take(d, h):
            slot = h * ROWS + d
            row_copy(send.at[slot], send.at[slot], phase, d, h, slot, slot).wait_send()

        others(take)

    def left(chain, send, phase):
        def take(d):
            slot = chain * ROWS + d
            row_copy(send.at[slot], send.at[slot], phase, d, chain, slot, slot).wait_send()

        def body(t, _):
            take(row_to(t))
            return 0

        lax.fori_loop(1, ROWS, body, 0)

        @pl.when(core != chain)
        def _():
            take(me)

    def strided(i):
        return pl.ds(i, TILE, stride=PART)

    low = lax.rem(lax.broadcasted_iota(jnp.int32, (TILE, TILE), 0), 8) < 4

    def halves(a, b):
        return (
            jnp.where(low, a, pltpu.roll(b, 4, 0)),
            jnp.where(low, pltpu.roll(a, TILE - 4, 0), b),
        )

    def four_of(recv, base, q):
        block = recv[:, pl.ds(pl.multiple_of(base + 16 * q, 16), 16), :].astype(F32)
        result = []
        for n in range(2):
            part = block[:, 8 * n : 8 * n + 8, :]
            a, b = part[0:ROWS].reshape(TILE, TILE), part[ROWS:].reshape(TILE, TILE)
            result += [m.astype(BF16) for m in halves(a, b)]
        return result

    def put_four(send, base, q, four):
        first, second = halves(four[0], four[1]), halves(four[2], four[3])
        where = pl.ds(pl.multiple_of(base + 16 * q, 16), 16)
        for h in range(2):
            both = [m[h].reshape(ROWS, 8, TILE) for m in (first, second)]
            send[h * ROWS : h * ROWS + ROWS, where, :] = jnp.concatenate(both, axis=1).astype(BF16)

    def fours(body):
        def step(q, _):
            body(q)
            return 0

        lax.fori_loop(0, 2, step, 0)

    def forward_channels(u, recv, send):
        def body(q):
            left, right = four_of(recv, 0, q), four_of(recv, 32, q)
            result = []
            for n in range(4):
                ch_l[u, 4 * q + n] = left[n]
                ch_r[u, 4 * q + n] = right[n]
                result.append(nt(left[n], right[n]) if u == 0 else tn(left[n], right[n]))
            put_four(send, 0, q, result)

        fours(body)

    def backward_channels(u, recv, send):
        def body(q):
            grads = four_of(recv, 0, q)
            lefts, rights = [], []
            for n in range(4):
                left, right, grad = ch_l[u, 4 * q + n], ch_r[u, 4 * q + n], grads[n]
                if u == 0:
                    lefts.append(nn(grad, right))
                    rights.append(tn(grad, left))
                else:
                    lefts.append(nt(right, grad))
                    rights.append(nn(left, grad))
            put_four(send, 0, q, lefts)
            put_four(send, 32, q, rights)

        fours(body)

    def front(u, i, chain, part, x):
        standard, inv_std = normalize(x)
        std[u, i] = standard
        inv[u, i] = inv_std
        normed = (standard * ngain[u]).astype(BF16)
        nrm[u, :, lanes(i)] = normed
        projected = nn(wt[u], normed)
        pair_mask = rowm[i] * masks[chain].astype(F32)
        s = jax.nn.sigmoid(projected[0:128])
        left = s * projected[128:256] * pair_mask
        cf[u, 0, i] = left * (1.0 - s)
        cf[u, 1, i] = s * pair_mask
        s_a[chain, strided(part), :] = left
        t = jax.nn.sigmoid(projected[256:384])
        right = t * projected[384:512] * pair_mask
        cf[u, 2, i] = right * (1.0 - t)
        cf[u, 3, i] = t * pair_mask
        s_b[chain, strided(part), :] = right
        gate[u, i] = jax.nn.sigmoid(projected[512:640])

    def finish(u, i, chain, part):
        prod_hat, mid_inv = normalize(s_a[chain, strided(part), :])
        middle = (prod_hat * mgain[u]).astype(BF16)
        update = nn(ft[u], middle)
        ph[u, i] = prod_hat
        minv[u, i] = mid_inv
        mdl[u, :, lanes(i)] = middle
        upd[u, i] = update
        return update, prod_hat, mid_inv

    def upper(u, i, chain, part, incoming, update, prod_hat, mid_inv, final):
        g = gate[u, i]
        inc[u, i] = incoming
        grad_update = (g * incoming).astype(BF16)
        gup[u, :, lanes(i)] = grad_update
        gproj[u, 512:640, lanes(i)] = (incoming * update * g * (1.0 - g)).astype(BF16)
        grad_middle = nn(final[...], grad_update)
        macc[u] += grad_middle * prod_hat
        s_b[chain, strided(part), :] = norm_back(grad_middle * mgain[u], prod_hat, mid_inv)

    def lower(u, i, chain, part, weight):
        grad_left, grad_right = s_a[chain, strided(part), :], s_b[chain, strided(part), :]
        gproj[u, 0:128, lanes(i)] = (grad_left * cf[u, 0, i]).astype(BF16)
        gproj[u, 128:256, lanes(i)] = (grad_left * cf[u, 1, i]).astype(BF16)
        gproj[u, 256:384, lanes(i)] = (grad_right * cf[u, 2, i]).astype(BF16)
        gproj[u, 384:512, lanes(i)] = (grad_right * cf[u, 3, i]).astype(BF16)
        grad_normed = nn(weight[...], gproj[u, :, lanes(i)])
        standard = std[u, i]
        gacc[u] += grad_normed * standard
        back = norm_back(grad_normed * ngain[u], standard, inv[u, i])
        return (inc[u, i] + back).astype(BF16)

    def spread(row):
        return jnp.broadcast_to(row[...], (TILE, TILE)).T

    def weights(u, w, n):
        for g in range(5):
            wt[u, g * 128 : g * 128 + 128, :] = turn(w[:, g * 128 : g * 128 + 128])
        ngain[u] = spread(n)

    for load in loads[0:4]:
        load.wait()
    weights(0, w1, n1)
    where = lax.broadcasted_iota(jnp.int32, (1, TILE), 1)

    def row_masks(chain):
        col_mask = masks[chain].astype(F32)
        for i in range(PART):
            here = where == me * OWN + core * PART + i
            picked = jnp.sum(jnp.where(here, col_mask, 0.0), axis=1, keepdims=True)
            rowm[chain * PART + i] = jnp.broadcast_to(picked, (1, TILE))

    row_masks(core)
    pl.semaphore_wait(barrier, 2 * (ROWS - 1) + groups - 1)
    swaps = [
        swap(0, pm_in.at[0, theirs], pm.at[mine]),
        swap(1, mask_in, masks.at[core]),
        swap(2, ct_in.at[0, theirs], ct.at[mine]),
    ]
    for copy in swaps:
        copy.start()

    def first(i, chain, part):
        x = pm[i].astype(F32).T
        xt[i] = x
        front(0, i, chain, part, x)

    def scatter_first(chain):
        scatter(chain, (s_a, s_b), send2.at[0], recv2.at[0], 0)

    tiles(core, first)

    @pl.when(core == 0)
    def _():
        scatter_first(0)

    swaps[0].wait()
    swaps[1].wait()
    row_masks(mate)
    tiles(mate, first)

    @pl.when(core == 1)
    def _():
        scatter_first(0)

    left(0, send2.at[0], 0)
    scatter_first(1)
    for load in loads[4:]:
        load.wait()
    swaps[2].wait()
    weights(1, w2, n2)
    for u, (f, m) in enumerate(((f1, m1), (f2, m2))):
        ft[u] = turn(f[...])
        mgain[u] = spread(m)
        gacc[u] = jnp.zeros((TILE, TILE), F32)
        macc[u] = jnp.zeros((TILE, TILE), F32)
    gathered(recv2.at[0], 0)
    forward_channels(0, recv2.at[0], send1.at[0])
    give_back(send1.at[0], recv1.at[0], 1)
    left(1, send2.at[0], 0)

    def second(i, chain, part):
        update, _, _ = finish(0, i, chain, part)
        first_out = (xt[i] + gate[0, i] * update).astype(BF16)
        front(1, i, chain, part, first_out.astype(F32))

    for chain in range(2):
        returned(chain, recv1.at[0], 1, (s_a,))
        tiles(chain, second)
        if chain == 1:
            left(0, send2.at[1], 2)
        scatter(chain, (s_a, s_b), send2.at[1], recv2.at[1], 2)
    sent(send1.at[0], 1)
    gathered(recv2.at[1], 2)
    forward_channels(1, recv2.at[1], send1.at[1])
    give_back(send1.at[1], recv1.at[1], 3)
    left(1, send2.at[1], 2)

    def third(i, chain, part):
        update, prod_hat, mid_inv = finish(1, i, chain, part)
        upper(1, i, chain, part, ct[i].astype(F32).T, update, prod_hat, mid_inv, f2)

    for chain in range(2):
        returned(chain, recv1.at[1], 3, (s_a,))
        tiles(chain, third)
        if chain == 1:
            left(0, send1.at[2], 4)
        scatter(chain, (s_b,), send1.at[2], recv1.at[2], 4)
    sent(send1.at[1], 3)
    pay[640:768, :] = nt(mdl[1], gup[1])
    gathered(recv1.at[2], 4)
    backward_channels(1, recv1.at[2], send2.at[2])
    give_back(send2.at[2], recv2.at[2], 5)
    left(1, send1.at[2], 4)

    def fourth(i, chain, part):
        first_grad = lower(1, i, chain, part, w2).astype(F32)
        upper(0, i, chain, part, first_grad, upd[0, i], ph[0, i], minv[0, i], f1)

    for chain in range(2):
        returned(chain, recv2.at[2], 5, (s_a, s_b))
        tiles(chain, fourth)
        if chain == 1:
            left(0, send1.at[3], 6)
        scatter(chain, (s_b,), send1.at[3], recv1.at[3], 6)
    sent(send2.at[2], 5)

    def vectors(values):
        vec[...] = jnp.zeros(vec.shape, F32)
        for n, value in enumerate(values):
            vec[n : n + 1, :] = jnp.sum(value.T, axis=0, keepdims=True)

    def blocks_out(send, recv, phase, block):
        def fill(d, ref):
            ref[d, 0:block, :] = pay[pl.ds(pl.multiple_of(d * block, block), block), :].astype(BF16)
            ref[d, block : block + 16, :] = vec[...].astype(BF16)

        fill(mq, recv)

        def body(t, _):
            d = grp_to(t)
            fill(d, send)
            grp_copy(send.at[d], recv.at[mq], phase, d, mq).start()
            return 0

        lax.fori_loop(1, groups, body, 0)

    def blocks_in(send, recv, phase):
        def body(t, _):
            s = grp_from(t)
            grp_copy(send.at[s], recv.at[s], phase, s, s).wait()
            return 0

        lax.fori_loop(1, groups, body, 0)
        return jnp.sum(recv[...].astype(F32), axis=0)

    def whole_out(value, send, recv, phase):
        send[...] = value.astype(BF16)
        recv[me] = value.astype(BF16)

        def body(t, _):
            d = row_to(t)
            row_copy(send, recv.at[me], phase, d, core, d, me).start()
            return 0

        lax.fori_loop(1, ROWS, body, 0)

    def whole_in(send, recv, phase):
        def body(t, _):
            s = row_from(t)
            row_copy(send, recv.at[s], phase, s, core, s, s).wait()
            return 0

        lax.fori_loop(1, ROWS, body, 0)
        return jnp.sum(recv[...].astype(F32), axis=0)

    def back_out(value, send, recv, phase):
        send[...] = value.astype(BF16)
        recv[mq] = value.astype(BF16)

        def body(t, _):
            d = grp_to(t)
            grp_copy(send, recv.at[mq], phase, d, mq).start()
            return 0

        lax.fori_loop(1, groups, body, 0)

    def back_in(send, recv, phase):
        def body(t, _):
            s = grp_from(t)
            grp_copy(send, recv.at[s], phase, s, s).wait()
            return 0

        lax.fori_loop(1, groups, body, 0)

    proj = nt(nrm[1], gproj[1])
    for g in range(5):
        pay[g * 128 : g * 128 + 128, :] = proj[:, g * 128 : g * 128 + 128]
    pay[768:896, :] = nt(mdl[0], gup[0])
    pay[896:1024, :] = nt(nrm[0], gproj[0, 512:640, :])
    vectors((gacc[1], macc[1], macc[0]))
    blocks_out(a2s, a2r, 8, 64)

    gathered(recv1.at[3], 6)
    backward_channels(0, recv1.at[3], send2.at[3])
    give_back(send2.at[3], recv2.at[3], 7)
    left(1, send1.at[3], 6)
    whole_out(blocks_in(a2s, a2r, 8), b2s, b2r, 9)

    def fifth(i, chain, part):
        out[i] = lower(0, i, chain, part, w1).astype(F32).T.astype(BF16)

    for chain in range(2):
        returned(chain, recv2.at[3], 7, (s_a, s_b))
        tiles(chain, fifth)
    sent(send2.at[3], 7)
    stores = [pltpu.make_async_copy(out.at[mine], out_to.at[0, mine], osem.at[0])]
    stores[0].start()
    swap_back = swap(3, out.at[theirs], out_to.at[0, mine])
    swap_back.start()

    def store(n, a, b):
        stores.append(pltpu.make_async_copy(a, b, osem.at[n]))
        stores[-1].start()

    proj = nt(nrm[0], gproj[0, 0:512, :])
    for g in range(4):
        pay[g * 128 : g * 128 + 128, :] = proj[:, g * 128 : g * 128 + 128]
    vectors((gacc[0],))
    blocks_out(a1s, a1r, 11, 32)

    total = whole_in(b2s, b2r, 9)
    back_out(total[0:64], c2s, c2r, 10)
    o_n2[...] = total[64:65] * factor
    o_m2[...] = total[65:66] * factor
    o_m1[...] = total[66:67] * factor
    store(1, o_n2, n2_to)
    store(2, o_m2, m2_to)
    store(3, o_m1, m1_to)

    whole_out(blocks_in(a1s, a1r, 11), b1s, b1r, 12)
    back_in(c2s, c2r, 10)
    sums = c2r[...].reshape(1024, TILE).astype(F32) * factor
    for g in range(5):
        o_p2[:, g * 128 : g * 128 + 128] = sums[g * 128 : g * 128 + 128]
    o_f2[...] = sums[640:768]
    o_f1[...] = sums[768:896]
    o_p1[:, 512:640] = sums[896:1024]
    store(4, o_p2, p2_to)
    store(5, o_f2, f2_to)
    store(6, o_f1, f1_to)

    total = whole_in(b1s, b1r, 12)
    back_out(total[0:32], c1s, c1r, 13)
    o_n1[...] = total[32:33] * factor
    store(7, o_n1, n1_to)
    back_in(c1s, c1r, 13)
    sums = c1r[...].reshape(512, TILE).astype(F32) * factor
    for g in range(4):
        o_p1[:, g * 128 : g * 128 + 128] = sums[g * 128 : g * 128 + 128]

    store(8, o_p1, p1_to)
    for copy in stores:
        copy.wait()
    swap_back.wait()


def hand_on(*refs):
    froms, tos, held, sems = refs[:9], refs[9:18], refs[18:27], refs[27]
    loads = [pltpu.make_async_copy(a, b, sems.at[0, n]) for n, (a, b) in enumerate(zip(froms, held))]
    stores = [pltpu.make_async_copy(a, b, sems.at[1, n]) for n, (a, b) in enumerate(zip(held, tos))]
    for load in loads:
        load.start()
    for load, store in zip(loads, stores):
        load.wait()
        store.start()
    for store in stores:
        store.wait()


def on_device(groups, factor, pm, ct, mask, n1, w1, m1, f1, n2, w2, m2, f2):
    wide = (1, TILE)
    shapes = [
        (pm.shape, BF16),
        (wide, F32), ((TILE, 640), F32), (wide, F32), ((TILE, TILE), F32),
        (wide, F32), ((TILE, 640), F32), (wide, F32), ((TILE, TILE), F32),
    ]
    tile = (OWN, TILE, TILE)
    lane = (TILE, OWN * TILE)
    loaded = [
        (pm.shape[1:], BF16), (ct.shape[1:], BF16), ((2,) + mask.shape, jnp.int32),
        (wide, F32), ((TILE, 640), BF16), (wide, F32), ((TILE, TILE), BF16),
        (wide, F32), ((TILE, 640), BF16), (wide, F32), ((TILE, TILE), BF16),
    ]
    scratch = [pltpu.VMEM(s, d) for s, d in loaded + [(pm.shape[1:], BF16)] + shapes[1:]] + [
        pltpu.VMEM((2, 640, TILE), BF16),
        pltpu.VMEM((2, TILE, TILE), BF16),
        pltpu.VMEM((2, TILE, TILE), F32),
        pltpu.VMEM((2, TILE, TILE), F32),
        pltpu.VMEM((OWN, 1, TILE), F32),
        pltpu.VMEM(tile, F32),
        pltpu.VMEM((2,) + tile, F32),
        pltpu.VMEM((2, OWN, 1, TILE), F32),
        pltpu.VMEM((2,) + lane, BF16),
        pltpu.VMEM((2, 4) + tile, F32),
        pltpu.VMEM((2,) + tile, F32),
        pltpu.VMEM((2,) + tile, F32),
        pltpu.VMEM((2, OWN, 1, TILE), F32),
        pltpu.VMEM((2,) + lane, BF16),
        pltpu.VMEM((2,) + tile, F32),
        pltpu.VMEM((2,) + lane, BF16),
        pltpu.VMEM((2, 640, OWN * TILE), BF16),
        pltpu.VMEM((2,) + tile, F32),
        pltpu.VMEM((2, PART * TILE, TILE), F32),
        pltpu.VMEM((2, PART * TILE, TILE), F32),
        pltpu.VMEM((2,) + tile, BF16),
        pltpu.VMEM((2,) + tile, BF16),
        pltpu.VMEM((2, TILE, TILE), F32),
        pltpu.VMEM((2, TILE, TILE), F32),
        pltpu.VMEM((1024, TILE), F32),
        pltpu.VMEM((16, TILE), F32),
        pltpu.VMEM((4, 2 * ROWS, 64, TILE), BF16),
        pltpu.VMEM((4, 2 * ROWS, 64, TILE), BF16),
        pltpu.VMEM((4, 2 * ROWS, 32, TILE), BF16),
        pltpu.VMEM((4, 2 * ROWS, 32, TILE), BF16),
        pltpu.VMEM((16, 80, TILE), BF16),
        pltpu.VMEM((16, 80, TILE), BF16),
        pltpu.VMEM((80, TILE), BF16),
        pltpu.VMEM((ROWS, 80, TILE), BF16),
        pltpu.VMEM((64, TILE), BF16),
        pltpu.VMEM((16, 64, TILE), BF16),
        pltpu.VMEM((16, 48, TILE), BF16),
        pltpu.VMEM((16, 48, TILE), BF16),
        pltpu.VMEM((48, TILE), BF16),
        pltpu.VMEM((ROWS, 48, TILE), BF16),
        pltpu.VMEM((32, TILE), BF16),
        pltpu.VMEM((16, 32, TILE), BF16),
        pltpu.SemaphoreType.DMA((14, 2 * ROWS)),
        pltpu.SemaphoreType.DMA((14, 2 * ROWS)),
        pltpu.SemaphoreType.DMA((11,)),
        pltpu.SemaphoreType.DMA((9,)),
        pltpu.SemaphoreType.DMA((4,)),
        pltpu.SemaphoreType.DMA((4,)),
    ]
    anywhere = pl.BlockSpec(memory_space=pl.ANY)
    results = pl.pallas_call(
        functools.partial(kernel, groups, factor),
        out_shape=[jax.ShapeDtypeStruct(s, d) for s, d in shapes],
        in_specs=[anywhere] * 11,
        out_specs=[anywhere] * 9,
        scratch_shapes=scratch,
        compiler_params=pltpu.CompilerParams(
            collective_id=0, has_side_effects=True, vmem_limit_bytes=VMEM_BYTES
        ),
        name="triangle",
    )(
        pm, ct, mask,
        n1.reshape(wide), w1, m1.reshape(wide), f1,
        n2.reshape(wide), w2, m2.reshape(wide), f2,
    )
    results = pl.pallas_call(
        hand_on,
        out_shape=[jax.ShapeDtypeStruct(s, d) for s, d in shapes],
        in_specs=[anywhere] * 9,
        out_specs=[anywhere] * 9,
        scratch_shapes=[pltpu.VMEM(s, d) for s, d in shapes] + [pltpu.SemaphoreType.DMA((2, 9))],
        compiler_params=pltpu.CompilerParams(vmem_limit_bytes=VMEM_BYTES),
        name="hand_on",
    )(*results)
    flat = [r.reshape(TILE) if r.shape == wide else r for r in results]
    return tuple(flat)


def solution(mesh):
    groups = mesh.shape["rep"] * mesh.shape["cplx"]
    factor = 1.0 / math.sqrt(groups * TILE * TILE)
    blocks = P(("rep", "cplx"), "row", None, None)
    placed = (blocks, blocks, P(("rep", "cplx"), None)) + (P(),) * 8
    return jax.shard_map(
        functools.partial(on_device, groups, factor),
        mesh=mesh,
        in_specs=placed,
        out_specs=(blocks,) + (P(),) * 8,
        check_vma=False,
    )
```

time: 132 us -> 123 us (0.932)
  Pallas kernels: 131 us -> 122 us
    pallas_call x1, Pallas kernels: 129 us -> 120 us  [on_device(): pl.pallas_call(functools.partial(kernel, groups, factor), out_shape=[jax....]
where the time goes in v3:
time: 123 us
  Pallas kernels  122 us (99%)
    pallas_call x1, Pallas kernels, on_device(): pl.pallas_call(functools.partial(kernel, groups, factor), out_shape=[jax....  120 us

profile of v3, /device:TPU:1, one launch (start us, length us, event | category | flops | bytes accessed | tf_op | source)
XLA Modules:
  0.0 123.0 jit_solution(2899901226473235375)
XLA Ops:
  0.6 120.2 %triangle.1 = (bf16[1,8,128,128]{3,2,1,0:T(8,128)(2,1)}, f32[1,128]{1,0:T(1,128)}, f32[128,640]{1,0:T(8,128)}, f32[1,128]{1,0:T(1,128)}, f32[128,128]{1,0:T(8,12...) custom-call(bf16[1,8,128,128]{3,2,1,0:T(8,128)(2,1)} %pm_in.1, ...), custom_call_target="tpu_custom_call" | custom-call | tf_op jit(solution)/shard_map/triangle/pallas_call | solution.py:716
  120.9 2.1 %hand_on.1 = (bf16[1,8,128,128]{3,2,1,0:T(8,128)(2,1)}, f32[1,128]{1,0:T(1,128)}, f32[128,640]{1,0:T(8,128)}, f32[1,128]{1,0:T(1,128)}, f32[128,128]{1,0:T(8,128...) custom-call(bf16[1,8,128,128]{3,2,1,0:T(8,128)(2,1)} %get-tuple-element.27.refs_0_, ...), custom_call_target="tpu_custom_call" | custom-call | tf_op jit(solution)/shard_map/hand_on/pallas_call | solution.py:731

commit v4 on v3

--- a/solution.py
+++ b/solution.py
@@ -61,7 +61,7 @@
     gacc, macc, pay, vec,
     send2, recv2, send1, recv1,
     a2s, a2r, b2s, b2r, c2s, c2r, a1s, a1r, b1s, b1r, c1s, c1r,
-    ssem, rsem, isem, osem, xsem, ysem,
+    ssem, rsem, gssem, grsem, isem, osem, xsem, ysem,
 ):
     me = lax.axis_index("row")
     my_x, my_z = me // 8, lax.rem(me, 8)
@@ -134,15 +134,18 @@
             src_ref=src, dst_ref=dst, send_sem=xsem.at[n], recv_sem=ysem.at[n],
             device_id=row_id(me, mate), device_id_type=MESH)
 
-    def row_copy(src, dst, phase, d, h, n, slot):
+    def row_copy(src, dst, send_sem, recv_sem, d, h):
         return pltpu.make_async_remote_copy(
-            src_ref=src, dst_ref=dst, send_sem=ssem.at[phase, n], recv_sem=rsem.at[phase, slot],
+            src_ref=src, dst_ref=dst, send_sem=send_sem, recv_sem=recv_sem,
             device_id=row_id(d, h), device_id_type=MESH)
 
-    def grp_copy(src, dst, phase, d, slot):
+    def grp_copy(src, dst, send_sem, recv_sem, d):
         return pltpu.make_async_remote_copy(
-            src_ref=src, dst_ref=dst, send_sem=ssem.at[phase, d], recv_sem=rsem.at[phase, slot],
+            src_ref=src, dst_ref=dst, send_sem=send_sem, recv_sem=recv_sem,
             device_id=grp_id(d), device_id_type=MESH)
+
+    def bytes_of(ref, sem):
+        pltpu.make_async_copy(ref, ref, sem).wait()
 
     def lanes(i):
         return pl.ds(pl.multiple_of(i * TILE, TILE), TILE)
@@ -155,17 +158,15 @@
         lax.fori_loop(0, PART, step, 0, unroll=4)
 
     def scatter(chain, stages, send, recv, phase):
-        def fill(d, slot, ref):
-            for n, stage in enumerate(stages):
-                ref[slot, n * 32 : n * 32 + 32, :] = stage[
-                    chain, pl.ds(pl.multiple_of(d * 32, 32), 32), :
-                ].astype(BF16)
+        base = chain * ROWS
+        mine_there = core * ROWS + me
+        for n, stage in enumerate(stages):
+            whole = stage[chain].reshape(ROWS, 32, TILE).astype(BF16)
+            send[pl.ds(base, ROWS), n * 32 : n * 32 + 32, :] = whole
 
         def post(d):
-            slot = chain * ROWS + d
-            fill(d, slot, send)
-            row_copy(send.at[slot], recv.at[core * ROWS + me], phase, d, chain, slot,
-                     core * ROWS + me).start()
+            row_copy(send.at[base + d], recv.at[mine_there], ssem.at[phase, chain],
+                     rsem.at[phase, 0], d, chain).start()
 
         def body(t, _):
             post(row_to(t))
@@ -175,95 +176,65 @@
 
         @pl.when(core == chain)
         def _():
-            fill(me, core * ROWS + me, recv)
+            recv[mine_there] = send[base + me]
 
         @pl.when(core != chain)
         def _():
             post(me)
 
-    def others(body):
-        def step(t, _):
-            d = row_to(t)
-            body(d, 0)
-            body(d, 1)
-            return 0
-
-        lax.fori_loop(1, ROWS, step, 0)
-        body(me, mate)
-
-    def give_back(send, recv, phase):
-        def post(d, h):
-            slot = h * ROWS + d
-            row_copy(send.at[slot], recv.at[core * ROWS + me], phase, d, h, slot,
-                     core * ROWS + me).start()
-
-        others(post)
-        recv[core * ROWS + me] = send[core * ROWS + me]
-
-    def others_from(body):
-        def step(t, _):
-            s = row_from(t)
-            body(s, 0)
-            body(s, 1)
-            return 0
-
-        lax.fori_loop(1, ROWS, step, 0)
-        body(me, mate)
-
-    def gathered(recv, phase):
-        def take(s, h):
-            slot = h * ROWS + s
-            row_copy(recv.at[slot], recv.at[slot], phase, s, h, slot, slot).wait_recv()
-
-        others_from(take)
-
-    def returned(chain, recv, phase, stages):
-        def take(s):
-            slot = chain * ROWS + s
-            for n, stage in enumerate(stages):
-                stage[chain, pl.ds(pl.multiple_of(s * 32, 32), 32), :] = recv[
-                    slot, n * 32 : n * 32 + 32, :
-                ].astype(F32)
-
-        def wait(s):
-            slot = chain * ROWS + s
-            row_copy(recv.at[slot], recv.at[slot], phase, s, chain, slot, slot).wait_recv()
+    def left(chain, send, phase):
+        @pl.when(core == chain)
+        def _():
+            bytes_of(send.at[0 : ROWS - 1], ssem.at[phase, chain])
 
         @pl.when(core != chain)
         def _():
-            wait(me)
-
-        take(me)
+            bytes_of(send.at[0:ROWS], ssem.at[phase, chain])
+
+    def give_back(send, recv, phase):
+        mine_there = core * ROWS + me
+
+        def post(d, h):
+            column = core * 2 + lax.rem(d // 8 + my_x, 2)
+            row_copy(send.at[h * ROWS + d], recv.at[mine_there], ssem.at[phase, 0],
+                     rsem.at[phase, column], d, h).start()
 
         def body(t, _):
-            s = row_from(t)
-            wait(s)
-            take(s)
+            d = row_to(t)
+            post(d, 0)
+            post(d, 1)
             return 0
 
         lax.fori_loop(1, ROWS, body, 0)
-
-    def sent(send, phase):
-        def take(d, h):
-            slot = h * ROWS + d
-            row_copy(send.at[slot], send.at[slot], phase, d, h, slot, slot).wait_send()
-
-        others(take)
-
-    def left(chain, send, phase):
-        def take(d):
-            slot = chain * ROWS + d
-            row_copy(send.at[slot], send.at[slot], phase, d, chain, slot, slot).wait_send()
-
-        def body(t, _):
-            take(row_to(t))
-            return 0
-
-        lax.fori_loop(1, ROWS, body, 0)
+        post(me, mate)
+        recv[mine_there] = send[mine_there]
+
+    def gave(send, phase):
+        bytes_of(send.at[0 : 2 * ROWS - 1], ssem.at[phase, 0])
+
+    def gathered(recv, phase):
+        bytes_of(recv.at[0 : 2 * ROWS - 1], rsem.at[phase, 0])
+
+    def returned(chain, recv, phase, stages):
+        def take(x):
+            slots = pl.ds(chain * ROWS + x * 8, 8)
+            rows = pl.ds(pl.multiple_of(x * 256, 256), 256)
+            for n, stage in enumerate(stages):
+                block = recv[slots, n * 32 : n * 32 + 32, :].astype(F32)
+                stage[chain, rows, :] = block.reshape(256, TILE)
+
+        bytes_of(recv.at[0:8], rsem.at[phase, chain * 2 + 1])
+        take(1 - my_x)
+
+        @pl.when(core == chain)
+        def _():
+            bytes_of(recv.at[0:7], rsem.at[phase, chain * 2])
 
         @pl.when(core != chain)
         def _():
-            take(me)
+            bytes_of(recv.at[0:8], rsem.at[phase, chain * 2])
+
+        take(my_x)
 
     def strided(i):
         return pl.ds(i, TILE, stride=PART)
@@ -460,7 +431,7 @@
         if chain == 1:
             left(0, send2.at[1], 2)
         scatter(chain, (s_a, s_b), send2.at[1], recv2.at[1], 2)
-    sent(send1.at[0], 1)
+    gave(send1.at[0], 1)
     gathered(recv2.at[1], 2)
     forward_channels(1, recv2.at[1], send1.at[1])
     give_back(send1.at[1], recv1.at[1], 3)
@@ -476,7 +447,7 @@
         if chain == 1:
             left(0, send1.at[2], 4)
         scatter(chain, (s_b,), send1.at[2], recv1.at[2], 4)
-    sent(send1.at[1], 3)
+    gave(send1.at[1], 3)
     pay[640:768, :] = nt(mdl[1], gup[1])
     gathered(recv1.at[2], 4)
     backward_channels(1, recv1.at[2], send2.at[2])
@@ -493,7 +464,7 @@
         if chain == 1:
             left(0, send1.at[3], 6)
         scatter(chain, (s_b,), send1.at[3], recv1.at[3], 6)
-    sent(send2.at[2], 5)
+    gave(send2.at[2], 5)
 
     def vectors(values):
         vec[...] = jnp.zeros(vec.shape, F32)
@@ -510,18 +481,14 @@
         def body(t, _):
             d = grp_to(t)
             fill(d, send)
-            grp_copy(send.at[d], recv.at[mq], phase, d, mq).start()
+            grp_copy(send.at[d], recv.at[mq], gssem.at[phase], grsem.at[phase], d).start()
             return 0
 
         lax.fori_loop(1, groups, body, 0)
 
     def blocks_in(send, recv, phase):
-        def body(t, _):
-            s = grp_from(t)
-            grp_copy(send.at[s], recv.at[s], phase, s, s).wait()
-            return 0
-
-        lax.fori_loop(1, groups, body, 0)
+        bytes_of(recv.at[0 : groups - 1], grsem.at[phase])
+        bytes_of(send.at[0 : groups - 1], gssem.at[phase])
         return jnp.sum(recv[...].astype(F32), axis=0)
 
     def whole_out(value, send, recv, phase):
@@ -530,18 +497,14 @@
 
         def body(t, _):
             d = row_to(t)
-            row_copy(send, recv.at[me], phase, d, core, d, me).start()
+            row_copy(send, recv.at[me], gssem.at[phase], grsem.at[phase], d, core).start()
             return 0
 
         lax.fori_loop(1, ROWS, body, 0)
 
-    def whole_in(send, recv, phase):
-        def body(t, _):
-            s = row_from(t)
-            row_copy(send, recv.at[s], phase, s, core, s, s).wait()
-            return 0
-
-        lax.fori_loop(1, ROWS, body, 0)
+    def whole_in(recv, phase):
+        bytes_of(recv.at[0 : ROWS - 1], grsem.at[phase])
+        bytes_of(recv.at[0 : ROWS - 1], gssem.at[phase])
         return jnp.sum(recv[...].astype(F32), axis=0)
 
     def back_out(value, send, recv, phase):
@@ -550,18 +513,14 @@
 
         def body(t, _):
             d = grp_to(t)
-            grp_copy(send, recv.at[mq], phase, d, mq).start()
+            grp_copy(send, recv.at[mq], gssem.at[phase], grsem.at[phase], d).start()
             return 0
 
         lax.fori_loop(1, groups, body, 0)
 
-    def back_in(send, recv, phase):
-        def body(t, _):
-            s = grp_from(t)
-            grp_copy(send, recv.at[s], phase, s, s).wait()
-            return 0
-
-        lax.fori_loop(1, groups, body, 0)
+    def back_in(recv, phase):
+        bytes_of(recv.at[0 : groups - 1], grsem.at[phase])
+        bytes_of(recv.at[0 : groups - 1], gssem.at[phase])
 
     proj = nt(nrm[1], gproj[1])
     for g in range(5):
@@ -569,13 +528,13 @@
     pay[768:896, :] = nt(mdl[0], gup[0])
     pay[896:1024, :] = nt(nrm[0], gproj[0, 512:640, :])
     vectors((gacc[1], macc[1], macc[0]))
-    blocks_out(a2s, a2r, 8, 64)
+    blocks_out(a2s, a2r, 0, 64)
 
     gathered(recv1.at[3], 6)
     backward_channels(0, recv1.at[3], send2.at[3])
     give_back(send2.at[3], recv2.at[3], 7)
     left(1, send1.at[3], 6)
-    whole_out(blocks_in(a2s, a2r, 8), b2s, b2r, 9)
+    whole_out(blocks_in(a2s, a2r, 0), b2s, b2r, 1)
 
     def fifth(i, chain, part):
         out[i] = lower(0, i, chain, part, w1).astype(F32).T.astype(BF16)
@@ -583,7 +542,7 @@
     for chain in range(2):
         returned(chain, recv2.at[3], 7, (s_a, s_b))
         tiles(chain, fifth)
-    sent(send2.at[3], 7)
+    gave(send2.at[3], 7)
     stores = [pltpu.make_async_copy(out.at[mine], out_to.at[0, mine], osem.at[0])]
     stores[0].start()
     swap_back = swap(3, out.at[theirs], out_to.at[0, mine])
@@ -597,10 +556,10 @@
     for g in range(4):
         pay[g * 128 : g * 128 + 128, :] = proj[:, g * 128 : g * 128 + 128]
     vectors((gacc[0],))
-    blocks_out(a1s, a1r, 11, 32)
-
-    total = whole_in(b2s, b2r, 9)
-    back_out(total[0:64], c2s, c2r, 10)
+    blocks_out(a1s, a1r, 3, 32)
+
+    total = whole_in(b2r, 1)
+    back_out(total[0:64], c2s, c2r, 2)
     o_n2[...] = total[64:65] * factor
     o_m2[...] = total[65:66] * factor
     o_m1[...] = total[66:67] * factor
@@ -608,8 +567,8 @@
     store(2, o_m2, m2_to)
     store(3, o_m1, m1_to)
 
-    whole_out(blocks_in(a1s, a1r, 11), b1s, b1r, 12)
-    back_in(c2s, c2r, 10)
+    whole_out(blocks_in(a1s, a1r, 3), b1s, b1r, 4)
+    back_in(c2r, 2)
     sums = c2r[...].reshape(1024, TILE).astype(F32) * factor
     for g in range(5):
         o_p2[:, g * 128 : g * 128 + 128] = sums[g * 128 : g * 128 + 128]
@@ -620,11 +579,11 @@
     store(5, o_f2, f2_to)
     store(6, o_f1, f1_to)
 
-    total = whole_in(b1s, b1r, 12)
-    back_out(total[0:32], c1s, c1r, 13)
+    total = whole_in(b1r, 4)
+    back_out(total[0:32], c1s, c1r, 5)
     o_n1[...] = total[32:33] * factor
     store(7, o_n1, n1_to)
-    back_in(c1s, c1r, 13)
+    back_in(c1r, 5)
     sums = c1r[...].reshape(512, TILE).astype(F32) * factor
     for g in range(4):
         o_p1[:, g * 128 : g * 128 + 128] = sums[g * 128 : g * 128 + 128]
@@ -705,8 +664,10 @@
         pltpu.VMEM((ROWS, 48, TILE), BF16),
         pltpu.VMEM((32, TILE), BF16),
         pltpu.VMEM((16, 32, TILE), BF16),
-        pltpu.SemaphoreType.DMA((14, 2 * ROWS)),
-        pltpu.SemaphoreType.DMA((14, 2 * ROWS)),
+        pltpu.SemaphoreType.DMA((8, 2)),
+        pltpu.SemaphoreType.DMA((8, 4)),
+        pltpu.SemaphoreType.DMA((6,)),
+        pltpu.SemaphoreType.DMA((6,)),
         pltpu.SemaphoreType.DMA((11,)),
         pltpu.SemaphoreType.DMA((9,)),
         pltpu.SemaphoreType.DMA((4,)),

time: 123 us -> 115 us (0.935)
  Pallas kernels: 122 us -> 114 us
    pallas_call x1, Pallas kernels: 120 us -> 112 us  [on_device(): pl.pallas_call(functools.partial(kernel, groups, factor), out_shape=[jax....]
where the time goes in v4:
time: 115 us
  Pallas kernels  114 us (99%)
    pallas_call x1, Pallas kernels, on_device(): pl.pallas_call(functools.partial(kernel, groups, factor), out_shape=[jax....  112 us

profile of v4, /device:TPU:1, one launch (start us, length us, event | category | flops | bytes accessed | tf_op | source)
XLA Modules:
  0.0 114.7 jit_solution(7504462472151258187)
XLA Ops:
  0.6 112.0 %triangle.1 = (bf16[1,8,128,128]{3,2,1,0:T(8,128)(2,1)}, f32[1,128]{1,0:T(1,128)}, f32[128,640]{1,0:T(8,128)}, f32[1,128]{1,0:T(1,128)}, f32[128,128]{1,0:T(8,12...) custom-call(bf16[1,8,128,128]{3,2,1,0:T(8,128)(2,1)} %pm_in.1, ...), custom_call_target="tpu_custom_call" | custom-call | tf_op jit(solution)/shard_map/triangle/pallas_call | solution.py:677
  112.6 2.1 %hand_on.1 = (bf16[1,8,128,128]{3,2,1,0:T(8,128)(2,1)}, f32[1,128]{1,0:T(1,128)}, f32[128,640]{1,0:T(8,128)}, f32[1,128]{1,0:T(1,128)}, f32[128,128]{1,0:T(8,128...) custom-call(bf16[1,8,128,128]{3,2,1,0:T(8,128)(2,1)} %get-tuple-element.27.refs_0_, ...), custom_call_target="tpu_custom_call" | custom-call | tf_op jit(solution)/shard_map/hand_on/pallas_call | solution.py:692

commit v5 on v4

--- a/solution.py
+++ b/solution.py
@@ -35,6 +35,10 @@
     return nn(turn(a), b)
 
 
+def sigmoid(a):
+    return 0.5 * jnp.tanh(0.5 * a) + 0.5
+
+
 def mean0(a):
     return jnp.mean(a, axis=0, keepdims=True)
 
@@ -52,7 +56,7 @@
 def kernel(
     groups, factor,
     pm_in, ct_in, mask_in, n1_in, w1_in, m1_in, f1_in, n2_in, w2_in, m2_in, f2_in,
-    out_to, n1_to, p1_to, m1_to, f1_to, n2_to, p2_to, m2_to, f2_to,
+    out_to, n1_to, p1_to, m1_to, f1_to, n2_to, p2_to, m2_to, f2_to, c1r,
     pm, ct, masks, n1, w1, m1, f1, n2, w2, m2, f2,
     out, o_n1, o_p1, o_m1, o_f1, o_n2, o_p2, o_m2, o_f2,
     wt, ft, ngain, mgain, rowm,
@@ -60,7 +64,7 @@
     s_a, s_b, ch_l, ch_r,
     gacc, macc, pay, vec,
     send2, recv2, send1, recv1,
-    a2s, a2r, b2s, b2r, c2s, c2r, a1s, a1r, b1s, b1r, c1s, c1r,
+    a2s, a2r, b2n, b2f, c2s, c2r, a1s, a1r, b1s, b1r, c1s,
     ssem, rsem, gssem, grsem, isem, osem, xsem, ysem,
 ):
     me = lax.axis_index("row")
@@ -126,8 +130,8 @@
     ]
     for load in loads:
         load.start()
-    lax.fori_loop(1, ROWS, greet_row, 0)
-    lax.fori_loop(1, groups, greet_grp, 0)
+    lax.fori_loop(1, ROWS, greet_row, 0, unroll=15)
+    lax.fori_loop(1, groups, greet_grp, 0, unroll=15)
 
     def swap(n, src, dst):
         return pltpu.make_async_remote_copy(
@@ -172,7 +176,7 @@
             post(row_to(t))
             return 0
 
-        lax.fori_loop(1, ROWS, body, 0)
+        lax.fori_loop(1, ROWS, body, 0, unroll=15)
 
         @pl.when(core == chain)
         def _():
@@ -205,7 +209,7 @@
             post(d, 1)
             return 0
 
-        lax.fori_loop(1, ROWS, body, 0)
+        lax.fori_loop(1, ROWS, body, 0, unroll=15)
         post(me, mate)
         recv[mine_there] = send[mine_there]
 
@@ -268,7 +272,7 @@
             body(q)
             return 0
 
-        lax.fori_loop(0, 2, step, 0)
+        lax.fori_loop(0, 2, step, 0, unroll=2)
 
     def forward_channels(u, recv, send):
         def body(q):
@@ -307,17 +311,17 @@
         nrm[u, :, lanes(i)] = normed
         projected = nn(wt[u], normed)
         pair_mask = rowm[i] * masks[chain].astype(F32)
-        s = jax.nn.sigmoid(projected[0:128])
+        s = sigmoid(projected[0:128])
         left = s * projected[128:256] * pair_mask
         cf[u, 0, i] = left * (1.0 - s)
         cf[u, 1, i] = s * pair_mask
         s_a[chain, strided(part), :] = left
-        t = jax.nn.sigmoid(projected[256:384])
+        t = sigmoid(projected[256:384])
         right = t * projected[384:512] * pair_mask
         cf[u, 2, i] = right * (1.0 - t)
         cf[u, 3, i] = t * pair_mask
         s_b[chain, strided(part), :] = right
-        gate[u, i] = jax.nn.sigmoid(projected[512:640])
+        gate[u, i] = sigmoid(projected[512:640])
 
     def finish(u, i, chain, part):
         prod_hat, mid_inv = normalize(s_a[chain, strided(part), :])
@@ -372,6 +376,15 @@
             rowm[chain * PART + i] = jnp.broadcast_to(picked, (1, TILE))
 
     row_masks(core)
+    def first(i, chain, part):
+        x = pm[i].astype(F32).T
+        xt[i] = x
+        front(0, i, chain, part, x)
+
+    def scatter_first(chain):
+        scatter(chain, (s_a, s_b), send2.at[0], recv2.at[0], 0)
+
+    tiles(core, first)
     pl.semaphore_wait(barrier, 2 * (ROWS - 1) + groups - 1)
     swaps = [
         swap(0, pm_in.at[0, theirs], pm.at[mine]),
@@ -380,16 +393,6 @@
     ]
     for copy in swaps:
         copy.start()
-
-    def first(i, chain, part):
-        x = pm[i].astype(F32).T
-        xt[i] = x
-        front(0, i, chain, part, x)
-
-    def scatter_first(chain):
-        scatter(chain, (s_a, s_b), send2.at[0], recv2.at[0], 0)
-
-    tiles(core, first)
 
     @pl.when(core == 0)
     def _():
@@ -484,7 +487,7 @@
             grp_copy(send.at[d], recv.at[mq], gssem.at[phase], grsem.at[phase], d).start()
             return 0
 
-        lax.fori_loop(1, groups, body, 0)
+        lax.fori_loop(1, groups, body, 0, unroll=15)
 
     def blocks_in(send, recv, phase):
         bytes_of(recv.at[0 : groups - 1], grsem.at[phase])
@@ -500,13 +503,33 @@
             row_copy(send, recv.at[me], gssem.at[phase], grsem.at[phase], d, core).start()
             return 0
 
-        lax.fori_loop(1, ROWS, body, 0)
+        lax.fori_loop(1, ROWS, body, 0, unroll=15)
 
     def whole_in(recv, phase):
         bytes_of(recv.at[0 : ROWS - 1], grsem.at[phase])
         bytes_of(recv.at[0 : ROWS - 1], gssem.at[phase])
         return jnp.sum(recv[...].astype(F32), axis=0)
 
+    def step_out(value, recv, step, phase):
+        mine_there, peers = step_peers(step)
+        recv[mine_there] = value.astype(BF16)
+        for d in peers:
+            row_copy(recv.at[mine_there], recv.at[mine_there], gssem.at[phase],
+                     grsem.at[phase], d, core).start()
+
+    def step_peers(step):
+        near, far = my_x * 2 + lax.rem(my_z, 2), my_z // 2
+        if step == 0:
+            spots = [lax.rem(near + t, 4) for t in range(1, 4)]
+            return near, [(p // 2) * 8 + far * 2 + lax.rem(p, 2) for p in spots]
+        spots = [lax.rem(far + t, 4) for t in range(1, 4)]
+        return far, [my_x * 8 + p * 2 + lax.rem(my_z, 2) for p in spots]
+
+    def step_in(recv, phase):
+        bytes_of(recv.at[0:3], grsem.at[phase])
+        bytes_of(recv.at[0:3], gssem.at[phase])
+        return jnp.sum(recv[...].astype(F32), axis=0)
+
     def back_out(value, send, recv, phase):
         send[...] = value.astype(BF16)
         recv[mq] = value.astype(BF16)
@@ -516,12 +539,15 @@
             grp_copy(send, recv.at[mq], gssem.at[phase], grsem.at[phase], d).start()
             return 0
 
-        lax.fori_loop(1, groups, body, 0)
+        lax.fori_loop(1, groups, body, 0, unroll=15)
 
     def back_in(recv, phase):
         bytes_of(recv.at[0 : groups - 1], grsem.at[phase])
         bytes_of(recv.at[0 : groups - 1], gssem.at[phase])
 
+    gathered(recv1.at[3], 6)
+    backward_channels(0, recv1.at[3], send2.at[3])
+    give_back(send2.at[3], recv2.at[3], 7)
     proj = nt(nrm[1], gproj[1])
     for g in range(5):
         pay[g * 128 : g * 128 + 128, :] = proj[:, g * 128 : g * 128 + 128]
@@ -530,11 +556,7 @@
     vectors((gacc[1], macc[1], macc[0]))
     blocks_out(a2s, a2r, 0, 64)
 
-    gathered(recv1.at[3], 6)
-    backward_channels(0, recv1.at[3], send2.at[3])
-    give_back(send2.at[3], recv2.at[3], 7)
     left(1, send1.at[3], 6)
-    whole_out(blocks_in(a2s, a2r, 0), b2s, b2r, 1)
 
     def fifth(i, chain, part):
         out[i] = lower(0, i, chain, part, w1).astype(F32).T.astype(BF16)
@@ -542,6 +564,8 @@
     for chain in range(2):
         returned(chain, recv2.at[3], 7, (s_a, s_b))
         tiles(chain, fifth)
+        if chain == 0:
+            step_out(blocks_in(a2s, a2r, 0), b2n, 0, 1)
     gave(send2.at[3], 7)
     stores = [pltpu.make_async_copy(out.at[mine], out_to.at[0, mine], osem.at[0])]
     stores[0].start()
@@ -557,8 +581,10 @@
         pay[g * 128 : g * 128 + 128, :] = proj[:, g * 128 : g * 128 + 128]
     vectors((gacc[0],))
     blocks_out(a1s, a1r, 3, 32)
-
-    total = whole_in(b2r, 1)
+    step_out(step_in(b2n, 1), b2f, 1, 6)
+
+    whole_out(blocks_in(a1s, a1r, 3), b1s, b1r, 4)
+    total = step_in(b2f, 6)
     back_out(total[0:64], c2s, c2r, 2)
     o_n2[...] = total[64:65] * factor
     o_m2[...] = total[65:66] * factor
@@ -566,43 +592,57 @@
     store(1, o_n2, n2_to)
     store(2, o_m2, m2_to)
     store(3, o_m1, m1_to)
-
-    whole_out(blocks_in(a1s, a1r, 3), b1s, b1r, 4)
+    total = whole_in(b1r, 4)
+    c1s[...] = total[0:32].astype(BF16)
+    own = pltpu.make_async_copy(c1s, c1r.at[mq], osem.at[9])
+    own.start()
+
+    def last(t, _):
+        grp_copy(c1s, c1r.at[mq], gssem.at[5], grsem.at[5], grp_to(t)).start()
+        return 0
+
+    lax.fori_loop(1, groups, last, 0, unroll=15)
+    o_n1[...] = total[32:33] * factor
+    store(7, o_n1, n1_to)
     back_in(c2r, 2)
     sums = c2r[...].reshape(1024, TILE).astype(F32) * factor
     for g in range(5):
         o_p2[:, g * 128 : g * 128 + 128] = sums[g * 128 : g * 128 + 128]
     o_f2[...] = sums[640:768]
     o_f1[...] = sums[768:896]
-    o_p1[:, 512:640] = sums[896:1024]
+    o_p1[...] = sums[896:1024]
     store(4, o_p2, p2_to)
     store(5, o_f2, f2_to)
     store(6, o_f1, f1_to)
-
-    total = whole_in(b1r, 4)
-    back_out(total[0:32], c1s, c1r, 5)
-    o_n1[...] = total[32:33] * factor
-    store(7, o_n1, n1_to)
-    back_in(c1r, 5)
-    sums = c1r[...].reshape(512, TILE).astype(F32) * factor
-    for g in range(4):
-        o_p1[:, g * 128 : g * 128 + 128] = sums[g * 128 : g * 128 + 128]
-
     store(8, o_p1, p1_to)
     for copy in stores:
         copy.wait()
+    own.wait()
     swap_back.wait()
-
-
-def hand_on(*refs):
-    froms, tos, held, sems = refs[:9], refs[9:18], refs[18:27], refs[27]
+    back_in(c1r, 5)
+
+
+def hand_on(factor, *refs):
+    froms, tos, held, sems = refs[:10], refs[10:19], refs[19:30], refs[30]
+    whole = held[10]
     loads = [pltpu.make_async_copy(a, b, sems.at[0, n]) for n, (a, b) in enumerate(zip(froms, held))]
-    stores = [pltpu.make_async_copy(a, b, sems.at[1, n]) for n, (a, b) in enumerate(zip(held, tos))]
+    last = 2
+    stores = [
+        pltpu.make_async_copy(whole if n == last else held[n], tos[n], sems.at[1, n])
+        for n in range(9)
+    ]
     for load in loads:
         load.start()
-    for load, store in zip(loads, stores):
-        load.wait()
-        store.start()
+    for n in range(9):
+        loads[n].wait()
+        if n != last:
+            stores[n].start()
+    loads[9].wait()
+    sums = held[9][...].reshape(512, TILE).astype(F32) * factor
+    for g in range(4):
+        whole[:, g * 128 : g * 128 + 128] = sums[g * 128 : g * 128 + 128]
+    whole[:, 512:640] = held[last][...]
+    stores[last].start()
     for store in stores:
         store.wait()
 
@@ -614,6 +654,8 @@
         (wide, F32), ((TILE, 640), F32), (wide, F32), ((TILE, TILE), F32),
         (wide, F32), ((TILE, 640), F32), (wide, F32), ((TILE, TILE), F32),
     ]
+    parts = list(shapes) + [((16, 32, TILE), BF16)]
+    parts[2] = ((TILE, TILE), F32)
     tile = (OWN, TILE, TILE)
     lane = (TILE, OWN * TILE)
     loaded = [
@@ -621,7 +663,7 @@
         (wide, F32), ((TILE, 640), BF16), (wide, F32), ((TILE, TILE), BF16),
         (wide, F32), ((TILE, 640), BF16), (wide, F32), ((TILE, TILE), BF16),
     ]
-    scratch = [pltpu.VMEM(s, d) for s, d in loaded + [(pm.shape[1:], BF16)] + shapes[1:]] + [
+    scratch = [pltpu.VMEM(s, d) for s, d in loaded + [(pm.shape[1:], BF16)] + parts[1:9]] + [
         pltpu.VMEM((2, 640, TILE), BF16),
         pltpu.VMEM((2, TILE, TILE), BF16),
         pltpu.VMEM((2, TILE, TILE), F32),
@@ -654,8 +696,8 @@
         pltpu.VMEM((4, 2 * ROWS, 32, TILE), BF16),
         pltpu.VMEM((16, 80, TILE), BF16),
         pltpu.VMEM((16, 80, TILE), BF16),
-        pltpu.VMEM((80, TILE), BF16),
-        pltpu.VMEM((ROWS, 80, TILE), BF16),
+        pltpu.VMEM((4, 80, TILE), BF16),
+        pltpu.VMEM((4, 80, TILE), BF16),
         pltpu.VMEM((64, TILE), BF16),
         pltpu.VMEM((16, 64, TILE), BF16),
         pltpu.VMEM((16, 48, TILE), BF16),
@@ -663,22 +705,21 @@
         pltpu.VMEM((48, TILE), BF16),
         pltpu.VMEM((ROWS, 48, TILE), BF16),
         pltpu.VMEM((32, TILE), BF16),
-        pltpu.VMEM((16, 32, TILE), BF16),
         pltpu.SemaphoreType.DMA((8, 2)),
         pltpu.SemaphoreType.DMA((8, 4)),
-        pltpu.SemaphoreType.DMA((6,)),
-        pltpu.SemaphoreType.DMA((6,)),
+        pltpu.SemaphoreType.DMA((7,)),
+        pltpu.SemaphoreType.DMA((7,)),
         pltpu.SemaphoreType.DMA((11,)),
-        pltpu.SemaphoreType.DMA((9,)),
+        pltpu.SemaphoreType.DMA((10,)),
         pltpu.SemaphoreType.DMA((4,)),
         pltpu.SemaphoreType.DMA((4,)),
     ]
     anywhere = pl.BlockSpec(memory_space=pl.ANY)
     results = pl.pallas_call(
         functools.partial(kernel, groups, factor),
-        out_shape=[jax.ShapeDtypeStruct(s, d) for s, d in shapes],
+        out_shape=[jax.ShapeDtypeStruct(s, d) for s, d in parts],
         in_specs=[anywhere] * 11,
-        out_specs=[anywhere] * 9,
+        out_specs=[anywhere] * 10,
         scratch_shapes=scratch,
         compiler_params=pltpu.CompilerParams(
             collective_id=0, has_side_effects=True, vmem_limit_bytes=VMEM_BYTES
@@ -690,11 +731,11 @@
         n2.reshape(wide), w2, m2.reshape(wide), f2,
     )
     results = pl.pallas_call(
-        hand_on,
+        functools.partial(hand_on, factor),
         out_shape=[jax.ShapeDtypeStruct(s, d) for s, d in shapes],
-        in_specs=[anywhere] * 9,
+        in_specs=[anywhere] * 10,
         out_specs=[anywhere] * 9,
-        scratch_shapes=[pltpu.VMEM(s, d) for s, d in shapes] + [pltpu.SemaphoreType.DMA((2, 9))],
+        scratch_shapes=[pltpu.VMEM(s, d) for s, d in parts + [shapes[2]]] + [pltpu.SemaphoreType.DMA((2, 10))],
         compiler_params=pltpu.CompilerParams(vmem_limit_bytes=VMEM_BYTES),
         name="hand_on",
     )(*results)

time: 115 us -> 111 us (0.965)
  Pallas kernels: 114 us -> 111 us
    pallas_call x1, Pallas kernels: 112 us -> 108 us  [on_device(): pl.pallas_call(functools.partial(kernel, groups, factor), out_shape=[jax....]
where the time goes in v5:
time: 111 us
  Pallas kernels  111 us (100%)
    pallas_call x1, Pallas kernels, on_device(): pl.pallas_call(functools.partial(kernel, groups, factor), out_shape=[jax....  108 us

profile of v5, /device:TPU:1, one launch (start us, length us, event | category | flops | bytes accessed | tf_op | source)
XLA Modules:
  0.0 111.3 jit_solution(13358949438317968076)
XLA Ops:
  0.6 108.4 %triangle.1 = (bf16[1,8,128,128]{3,2,1,0:T(8,128)(2,1)}, f32[1,128]{1,0:T(1,128)}, f32[128,128]{1,0:T(8,128)}, f32[1,128]{1,0:T(1,128)}, f32[128,128]{1,0:T(8,12...) custom-call(bf16[1,8,128,128]{3,2,1,0:T(8,128)(2,1)} %pm_in.1, ...), custom_call_target="tpu_custom_call" | custom-call | tf_op jit(solution)/shard_map/triangle/pallas_call | solution.py:718
  109.1 2.2 %hand_on.1 = (bf16[1,8,128,128]{3,2,1,0:T(8,128)(2,1)}, f32[1,128]{1,0:T(1,128)}, f32[128,640]{1,0:T(8,128)}, f32[1,128]{1,0:T(1,128)}, f32[128,128]{1,0:T(8,128...) custom-call(bf16[1,8,128,128]{3,2,1,0:T(8,128)(2,1)} %get-tuple-element.28.refs_0_, ...), custom_call_target="tpu_custom_call" | custom-call | tf_op jit(solution)/shard_map/hand_on/pallas_call | solution.py:733

commit v6 on v5

--- a/solution.py
+++ b/solution.py
@@ -168,15 +168,20 @@
             whole = stage[chain].reshape(ROWS, 32, TILE).astype(BF16)
             send[pl.ds(base, ROWS), n * 32 : n * 32 + 32, :] = whole
 
-        def post(d):
-            row_copy(send.at[base + d], recv.at[mine_there], ssem.at[phase, chain],
+        def post(d, n):
+            row_copy(send.at[base + d], recv.at[mine_there], ssem.at[phase, chain * 2 + n],
                      rsem.at[phase, 0], d, chain).start()
 
-        def body(t, _):
-            post(row_to(t))
+        def body_far(t, _):
+            post(row_to(t), 0)
             return 0
 
-        lax.fori_loop(1, ROWS, body, 0, unroll=15)
+        def body_near(t, _):
+            post(row_to(t), 1)
+            return 0
+
+        lax.fori_loop(1, 9, body_far, 0, unroll=8)
+        lax.fori_loop(9, ROWS, body_near, 0, unroll=7)
 
         @pl.when(core == chain)
         def _():
@@ -184,16 +189,24 @@
 
         @pl.when(core != chain)
         def _():
-            post(me)
-
-    def left(chain, send, phase):
+            post(me, 1)
+
+    def left_far(chain, send, phase):
+        bytes_of(send.at[0:8], ssem.at[phase, chain * 2])
+
+    def left_near(chain, send, phase):
         @pl.when(core == chain)
         def _():
-            bytes_of(send.at[0 : ROWS - 1], ssem.at[phase, chain])
+            bytes_of(send.at[0:7], ssem.at[phase, chain * 2 + 1])
 
         @pl.when(core != chain)
         def _():
-            bytes_of(send.at[0:ROWS], ssem.at[phase, chain])
+            bytes_of(send.at[0:8], ssem.at[phase, chain * 2 + 1])
+
+    def left(send, phase):
+        left_near(0, send, phase)
+        left_far(1, send, phase)
+        left_near(1, send, phase)
 
     def give_back(send, recv, phase):
         mine_there = core * ROWS + me
@@ -407,7 +420,7 @@
     def _():
         scatter_first(0)
 
-    left(0, send2.at[0], 0)
+    left_far(0, send2.at[0], 0)
     scatter_first(1)
     for load in loads[4:]:
         load.wait()
@@ -421,7 +434,7 @@
     gathered(recv2.at[0], 0)
     forward_channels(0, recv2.at[0], send1.at[0])
     give_back(send1.at[0], recv1.at[0], 1)
-    left(1, send2.at[0], 0)
+    left(send2.at[0], 0)
 
     def second(i, chain, part):
         update, _, _ = finish(0, i, chain, part)
@@ -432,13 +445,13 @@
         returned(chain, recv1.at[0], 1, (s_a,))
         tiles(chain, second)
         if chain == 1:
-            left(0, send2.at[1], 2)
+            left_far(0, send2.at[1], 2)
         scatter(chain, (s_a, s_b), send2.at[1], recv2.at[1], 2)
     gave(send1.at[0], 1)
     gathered(recv2.at[1], 2)
     forward_channels(1, recv2.at[1], send1.at[1])
     give_back(send1.at[1], recv1.at[1], 3)
-    left(1, send2.at[1], 2)
+    left(send2.at[1], 2)
 
     def third(i, chain, part):
         update, prod_hat, mid_inv = finish(1, i, chain, part)
@@ -448,14 +461,14 @@
         returned(chain, recv1.at[1], 3, (s_a,))
         tiles(chain, third)
         if chain == 1:
-            left(0, send1.at[2], 4)
+            left_far(0, send1.at[2], 4)
         scatter(chain, (s_b,), send1.at[2], recv1.at[2], 4)
     gave(send1.at[1], 3)
     pay[640:768, :] = nt(mdl[1], gup[1])
     gathered(recv1.at[2], 4)
     backward_channels(1, recv1.at[2], send2.at[2])
     give_back(send2.at[2], recv2.at[2], 5)
-    left(1, send1.at[2], 4)
+    left(send1.at[2], 4)
 
     def fourth(i, chain, part):
         first_grad = lower(1, i, chain, part, w2).astype(F32)
@@ -465,7 +478,7 @@
         returned(chain, recv2.at[2], 5, (s_a, s_b))
         tiles(chain, fourth)
         if chain == 1:
-            left(0, send1.at[3], 6)
+            left_far(0, send1.at[3], 6)
         scatter(chain, (s_b,), send1.at[3], recv1.at[3], 6)
     gave(send2.at[2], 5)
 
@@ -556,7 +569,7 @@
     vectors((gacc[1], macc[1], macc[0]))
     blocks_out(a2s, a2r, 0, 64)
 
-    left(1, send1.at[3], 6)
+    left(send1.at[3], 6)
 
     def fifth(i, chain, part):
         out[i] = lower(0, i, chain, part, w1).astype(F32).T.astype(BF16)
@@ -564,23 +577,24 @@
     for chain in range(2):
         returned(chain, recv2.at[3], 7, (s_a, s_b))
         tiles(chain, fifth)
+        half = slice(chain * 512, chain * 512 + 512)
+        proj = nt(nrm[0, :, half], gproj[0, 0:512, half])
+        for g in range(4):
+            rows = slice(g * 128, g * 128 + 128)
+            pay[rows, :] = proj[:, rows] if chain == 0 else pay[rows, :] + proj[:, rows]
         if chain == 0:
             step_out(blocks_in(a2s, a2r, 0), b2n, 0, 1)
+    def store(n, a, b):
+        stores.append(pltpu.make_async_copy(a, b, osem.at[n]))
+        stores[-1].start()
+
+    vectors((gacc[0],))
+    blocks_out(a1s, a1r, 3, 32)
     gave(send2.at[3], 7)
     stores = [pltpu.make_async_copy(out.at[mine], out_to.at[0, mine], osem.at[0])]
     stores[0].start()
     swap_back = swap(3, out.at[theirs], out_to.at[0, mine])
     swap_back.start()
-
-    def store(n, a, b):
-        stores.append(pltpu.make_async_copy(a, b, osem.at[n]))
-        stores[-1].start()
-
-    proj = nt(nrm[0], gproj[0, 0:512, :])
-    for g in range(4):
-        pay[g * 128 : g * 128 + 128, :] = proj[:, g * 128 : g * 128 + 128]
-    vectors((gacc[0],))
-    blocks_out(a1s, a1r, 3, 32)
     step_out(step_in(b2n, 1), b2f, 1, 6)
 
     whole_out(blocks_in(a1s, a1r, 3), b1s, b1r, 4)
@@ -705,7 +719,7 @@
         pltpu.VMEM((48, TILE), BF16),
         pltpu.VMEM((ROWS, 48, TILE), BF16),
         pltpu.VMEM((32, TILE), BF16),
-        pltpu.SemaphoreType.DMA((8, 2)),
+        pltpu.SemaphoreType.DMA((8, 4)),
         pltpu.SemaphoreType.DMA((8, 4)),
         pltpu.SemaphoreType.DMA((7,)),
         pltpu.SemaphoreType.DMA((7,)),

time: 111 us -> 111 us (level)
  no operation moved by 1% of the time
where the time goes in v6:
time: 111 us
  Pallas kernels  110 us (99%)
    pallas_call x1, Pallas kernels, on_device(): pl.pallas_call(functools.partial(kernel, groups, factor), out_shape=[jax....  108 us

profile of v6, /device:TPU:1, one launch (start us, length us, event | category | flops | bytes accessed | tf_op | source)
XLA Modules:
  0.0 110.9 jit_solution(5050044688246113535)
XLA Ops:
  0.6 108.1 %triangle.1 = (bf16[1,8,128,128]{3,2,1,0:T(8,128)(2,1)}, f32[1,128]{1,0:T(1,128)}, f32[128,128]{1,0:T(8,128)}, f32[1,128]{1,0:T(1,128)}, f32[128,128]{1,0:T(8,12...) custom-call(bf16[1,8,128,128]{3,2,1,0:T(8,128)(2,1)} %pm_in.1, ...), custom_call_target="tpu_custom_call" | custom-call | tf_op jit(solution)/shard_map/triangle/pallas_call | solution.py:732
  108.8 2.2 %hand_on.1 = (bf16[1,8,128,128]{3,2,1,0:T(8,128)(2,1)}, f32[1,128]{1,0:T(1,128)}, f32[128,640]{1,0:T(8,128)}, f32[1,128]{1,0:T(1,128)}, f32[128,128]{1,0:T(8,128...) custom-call(bf16[1,8,128,128]{3,2,1,0:T(8,128)(2,1)} %get-tuple-element.28.refs_0_, ...), custom_call_target="tpu_custom_call" | custom-call | tf_op jit(solution)/shard_map/hand_on/pallas_call | solution.py:747
